TPU v7x, 256 devices: a whole 4x4x8 slice. The times are simulated.
256 devices in a mesh: ctx: 32 (over z, x_lo, core), section: 8 (over y, x_hi).
Axes of the slice: x: 4 (x_hi: 2, x_lo: 2; x = x_hi * 2 + x_lo), y: 4, z: 8, core: 2. Of those that a mesh axis runs over, the one named last changes fastest.
Arguments:
- queries: bfloat16 [8, 8192, 4608], P('section', 'ctx'), may hold values from -32 to 32
- latent_cache: bfloat16 [8, 576, 8192], P('section', None, 'ctx'), may hold values from -4 to 4
- doc_ids: int32 [8, 8192], P('section', 'ctx'), may hold values from 0 to 7, never falling along the last dimension, each value on 1 to 6144 neighbouring positions
- block_table: int32 [32, 32], replicated, may hold values 0 or 1
- w_uv: bfloat16 [8, 8, 512, 128], P('section'), may hold values from -0.5 to 0.5
Outputs:
- handed: bfloat16 [8, 8192, 1024], P('section', 'ctx')
Inputs may be any that keep to these rules, and one draw needn't show every extreme that they name: `doc_ids`: along each layer's 8192 tokens the document ids never fall.
All inputs are finite; a program needn't handle non-finite values.
Results may differ from a plain program's by a relative error of at most 0.009.
Values may be sent and summed in bfloat16 or wider, within the bound.
No kernel may reach another device: no remote copies, remote signals or barrier semaphores. Data moves between devices by JAX's collectives and lax.ppermute only.
A program may use at most 64 MiB of HBM per device.

v0:
```python
import functools
import jax
import jax.numpy as jnp
from jax import lax
from jax.experimental import pallas as pl
from jax.experimental.pallas import tpu as pltpu
from jax.sharding import PartitionSpec as P

very_low = -1e30
log2_e = 1.4426950408889634
id_rows = 16
documents = 8


def dot(a, b, of_a, of_b):
    return lax.dot_general(a, b, (((of_a,), (of_b,)), ((), ())), preferred_element_type=jnp.float32)


def origin_of(me, place, e):
    step, across, swapped = place
    holder = me ^ (2 * across + swapped)
    if step == 0:
        return holder ^ e
    back = jnp.where((holder & 1) == 0, step, 7 - step)
    return (holder ^ e) - 4 * back


def attend(places, first, chosen, final, factor_scale, row, ids_s, ids_v, queries, *refs):
    pieces, refs = refs[: len(places)], refs[len(places) :]
    if final:
        up, refs = refs[0], refs[1:]
    if not first:
        refs = refs[3:]
    (peak, total, accum), refs = refs[:3], refs[3:]
    if final:
        out, refs = refs[0], refs[1:]
    flipped, turned, values, bias, score_buf, weight_buf, factor_buf = refs
    heads, latent, tokens = accum.shape
    width = queries.shape[0] // heads
    me = lax.axis_index("ctx")
    first_id = ids_s[0, 0]
    blocks = []
    for piece, place in zip(pieces, places):
        for e in range(piece.shape[0]):
            blocks.append((piece.at[e], place, e))
    if first:
        peak[...] = jnp.full(peak.shape, very_low, jnp.float32)
        total[...] = jnp.zeros(total.shape, jnp.float32)
        accum[...] = jnp.zeros(accum.shape, jnp.float32)
    query_ids = ids_v[...]
    key_at = lax.broadcasted_iota(jnp.int32, (tokens, tokens), 0)
    first_float = first_id.astype(jnp.float32)
    key_ids = [b[width : width + id_rows, :].astype(jnp.float32)[0:1, :] for b, _, _ in blocks]
    counts = [jnp.sum(jnp.where(k < first_float, 1.0, 0.0), axis=1, keepdims=True) for k in key_ids]
    befores = [c[0, 0].astype(jnp.int32) for c in counts]
    live_count = jnp.int32(0)
    for (block, place, e), ids_here, before in zip(blocks, key_ids, befores):
        own = place == (0, 0, 0) and e == 0
        origin = origin_of(me, place, e)
        if own:
            live = jnp.bool_(True)
        else:
            hit = row[0, jnp.maximum(origin, 0)]
            live = (origin >= 0) & (origin < me) & (hit == 1) & (before < tokens)

        def pack(block=block, ids_here=ids_here, before=before, slot=live_count, own=own):
            values[slot] = block[0:width, :]
            if own:
                start = jnp.zeros(query_ids.shape, jnp.int32)
                for d in range(documents):
                    below = jnp.sum(jnp.where(ids_here < float(d), 1.0, 0.0), axis=1, keepdims=True)
                    start = jnp.where(query_ids == d, below.astype(jnp.int32), start)
                query_at = lax.broadcasted_iota(jnp.int32, (tokens, tokens), 1)
                allowed = (key_at >= start) & (key_at <= query_at)
            else:
                allowed = (key_at >= before) & (query_ids == first_id)
            bias[slot] = jnp.where(allowed, 0.0, very_low)

        if own:
            pack()
        else:
            pl.when(live)(pack)
        live_count = live_count + live.astype(jnp.int32)

    spans = [slice(at, min(at + 128, width)) for at in range(0, width, 128)]
    count = len(chosen)
    shares = [spans[len(spans) * i // (count - 1) : len(spans) * (i + 1) // (count - 1)] for i in range(count - 1)]

    def score(slot, head, half):
        rows = queries[head * width : (head + 1) * width, :]
        score_buf[half] = dot(flipped[...], rows, 1, 0) + bias[slot]

    def weigh(head, half):
        scores = score_buf[half]
        old = peak[head : head + 1, :]
        new = jnp.maximum(old, jnp.max(scores, axis=0, keepdims=True))
        factor = jnp.exp2((old - new) * factor_scale)
        weights = jnp.exp2((scores - new) * factor_scale)
        total[head : head + 1, :] = total[head : head + 1, :] * factor + jnp.sum(weights, axis=0, keepdims=True)
        peak[head : head + 1, :] = new
        factor_buf[half] = jnp.broadcast_to(factor, factor_buf.shape[1:])
        weight_buf[half] = weights.astype(jnp.bfloat16)

    def mix(slot, head, half):
        accum[head] = accum[head] * factor_buf[half][0:1, :] + dot(values[slot, 0:latent, :], weight_buf[half], 1, 0)

    @pl.when(live_count > 0)
    def _():
        weight_buf[1] = jnp.zeros(weight_buf.shape[1:], weight_buf.dtype)
        factor_buf[1] = jnp.ones(factor_buf.shape[1:], factor_buf.dtype)
        flipped[...] = values[0].T
        score(0, chosen[0], 0)

        def over_live(slot, carry):
            after, prior = jnp.minimum(slot + 1, live_count - 1), jnp.maximum(slot - 1, 0)
            for i, head in enumerate(chosen):
                half = i % 2
                if i == count - 1:
                    flipped[...] = turned[...]
                score(slot if i < count - 1 else after, chosen[(i + 1) % count], 1 - half)
                weigh(head, half)
                mix(slot if i > 0 else prior, chosen[i - 1], 1 - half)
                if i < count - 1:
                    for span in shares[i]:
                        turned[:, span] = values[after, span, :].T
            return carry

        lax.fori_loop(0, live_count, over_live, 0)
        mix(live_count - 1, chosen[-1], (count - 1) % 2)

    if final:
        value_width = up.shape[2]
        for i, head in enumerate(chosen):
            mixed = (accum[head] / total[head : head + 1, :]).astype(jnp.bfloat16)
            part = dot(up[head], mixed, 0, 0)
            out[:, i * value_width : (i + 1) * value_width] = part.T.astype(jnp.bfloat16)


def stage(places, pieces, row, ids, queries, state, up, sizes, chosen=None):
    heads, latent, tokens, width, value_width = sizes
    first, final = state is None, up is not None
    chosen = tuple(range(heads)) if chosen is None else chosen
    count = sum(p.shape[0] for p in pieces)
    scalars, vectors = pl.BlockSpec(memory_space=pltpu.SMEM), pl.BlockSpec(memory_space=pltpu.VMEM)
    shapes = [((heads, tokens), jnp.float32), ((heads, tokens), jnp.float32), ((heads, latent, tokens), jnp.float32)]
    operands = [row, ids, ids, queries, *pieces]
    specs = [scalars, scalars, vectors, vectors] + [vectors] * len(pieces)
    aliases = {}
    out_shape = [pltpu.VMEM(shape, dtype) for shape, dtype in shapes]
    if final:
        operands.append(up)
        specs.append(vectors)
        out_shape.append(jax.ShapeDtypeStruct((tokens, len(chosen) * value_width), jnp.bfloat16))
    if not first:
        aliases = {len(operands) + i: i for i in range(3)}
        operands += [pltpu.with_memory_space_constraint(x, pltpu.VMEM) for x in state]
        specs += [vectors] * 3
    scratch = [
        pltpu.VMEM((tokens, width), jnp.bfloat16),
        pltpu.VMEM((tokens, width), jnp.bfloat16),
        pltpu.VMEM((count, width, tokens), jnp.bfloat16),
        pltpu.VMEM((count, tokens, tokens), jnp.float32),
        pltpu.VMEM((2, tokens, tokens), jnp.float32),
        pltpu.VMEM((2, tokens, tokens), jnp.bfloat16),
        pltpu.VMEM((2, 8, tokens), jnp.float32),
    ]
    scale = (value_width + width - latent) ** -0.5 * log2_e
    work = 2 * count * heads * tokens * tokens * (width + latent)
    result = pl.pallas_call(
        functools.partial(attend, tuple(places), first, chosen, final, scale),
        out_shape=out_shape,
        in_specs=specs,
        out_specs=[vectors] * len(out_shape),
        scratch_shapes=scratch,
        input_output_aliases=aliases,
        cost_estimate=pl.CostEstimate(
            flops=work, bytes_accessed=count * 2 * width * tokens, transcendentals=count * heads * tokens * tokens
        ),
        compiler_params=pltpu.CompilerParams(vmem_limit_bytes=24 * 2**20),
        name="attend",
    )(*operands)
    return list(result)


def tie(*arrays):
    return list(lax.optimization_barrier(tuple(arrays)))


def shards(queries, latent_cache, doc_ids, block_table, w_uv):
    tokens, heads, latent, value_width = queries.shape[1], w_uv.shape[1], w_uv.shape[2], w_uv.shape[3]
    width = latent_cache.shape[1]
    sizes = (heads, latent, tokens, width, value_width)
    devices = lax.axis_size("ctx")
    me = lax.axis_index("ctx")

    def across(x):
        return lax.ppermute(x, "ctx", [(i, i ^ 2) for i in range(devices)])

    def core(x):
        return lax.ppermute(x, "ctx", [(i, i ^ 1) for i in range(devices)])

    def along(x, step):
        down = 8 if step == 1 else 4
        return lax.ppermute(x, "ctx", [(i, (i + 4 if i % 2 == 0 else i - down) % devices) for i in range(devices)])

    ids = jnp.broadcast_to(doc_ids.astype(jnp.bfloat16), (id_rows, tokens))
    own = jnp.concatenate([latent_cache[0], ids], axis=0)[None]
    c0, x0 = core(own), across(own)
    row = lax.dynamic_slice_in_dim(block_table, me, 1, 0)

    pair = jnp.concatenate([own, c0], axis=0)
    z1 = along(pair, 1)
    queries_t = pltpu.with_memory_space_constraint(queries[0].T, pltpu.VMEM)

    def run(places, pieces, state, up=None, chosen=None):
        return stage(places, pieces, row, doc_ids, queries_t, state, up, sizes, chosen)

    state = run([(0, 0, 0)], [pair], None)
    *state, x0 = tie(*state, x0)
    cx0 = core(x0)
    state = run([(0, 1, 0)], [x0], state)
    *state, z1 = tie(*state, z1)
    z2, cz1, x1 = along(z1, 2), core(z1), across(z1)
    state = run([(0, 1, 1), (1, 0, 0)], [cx0, z1], state)
    *state, z2 = tie(*state, z2)
    z3, cz2 = along(z2, 3), core(z2)
    state = run([(1, 0, 1), (2, 0, 0)], [cz1, z2], state)
    *state, x1, z3 = tie(*state, x1, z3)
    x3, xz2, cx1, cz3 = across(z3), along(x1, 2), core(x1), core(z3)
    state = run([(2, 0, 1), (1, 1, 0)], [cz2, x1], state)
    state = run([(1, 1, 1), (3, 0, 0)], [cx1, z3], state)
    *state, xz2, x3 = tie(*state, xz2, x3)
    cxz2, cx3 = core(xz2), core(x3)
    state = run([(3, 0, 1)], [cz3], state)
    sections = lax.axis_size("section")
    handed = []
    for part in (tuple(range(heads - heads // 4)), tuple(range(heads - heads // 4, heads))):
        *state, heads_out = run(
            [(2, 1, 0), (2, 1, 1), (3, 1, 0), (3, 1, 1)], [xz2, cxz2, x3, cx3], state, w_uv[0], part
        )
        handed.append(lax.ppermute(heads_out[None], "section", [(i, (i + 1) % sections) for i in range(sections)]))
    return jnp.concatenate(handed, axis=2)


def solution(mesh):
    placed = (
        P("section", "ctx", None),
        P("section", None, "ctx"),
        P("section", "ctx"),
        P(),
        P("section", None, None, None),
    )
    return jax.shard_map(
        shards, mesh=mesh, in_specs=placed, out_specs=P("section", "ctx", None), check_vma=False
    )
```

profile of v0, /device:TPU:192, one launch (start us, length us, event | category | flops | bytes accessed | tf_op | source)
XLA Modules:
  0.0 97.1 jit_solution(3692224079941420115)
XLA Ops:
  0.0 0.0 copy-start
  0.0 0.0 copy-start.1
  0.0 0.8 convert_reduce_fusion
  0.8 1.7 %maximum_bitcast_fusion = bf16[1,592,256]{2,1,0:T(8,128)(2,1)} fusion(bf16[16,256]{1,0:T(8,128)(2,1)S(1)} %broadcast_in_dim.17, bf16[576,256]{1,0:T(8,128)(2,1)} %bitcast.22), kind=kLoop, calls=%fused_computation.2 | loop fusion | flops 606208 | bytes 606208 | tf_op jit(solution)/shard_map/broadcast_in_dim | solution.py:207
  2.5 0.0 collective-permute-start
  2.5 1.8 %collective-permute-done = bf16[1,592,256]{2,1,0:T(8,128)(2,1)S(1)} collective-permute-done((bf16[1,592,256]{2,1,0:T(8,128)(2,1)}, bf16[1,592,256]{2,1,0:T(8,128)(2,1)S(1)}, u32[]{:S(2)}, u32[]{:S(2)}) %collective-permute-start) | collective-permute-done | bytes 303136 | tf_op jit(solution)/shard_map/ppermute | solution.py:200
  4.3 1.0 %pad_maximum_fusion.refs_0_ = bf16[2,592,256]{2,1,0:T(8,128)(2,1)S(1)} fusion(bf16[1,592,256]{2,1,0:T(8,128)(2,1)S(1)} %collective-permute-done, bf16[1,592,256]{2,1,0:T(8,128)(2,1)} %maximum_bitcast_fusion), kind=kLoop, calls=%fused_computation | loop fusion | flops 303104 | bytes 1212416 | tf_op jit(solution)/shard_map/concatenate | solution.py:211
  5.3 1.1 %collective-permute-start.2 = (bf16[2,592,256]{2,1,0:T(8,128)(2,1)S(1)}, bf16[2,592,256]{2,1,0:T(8,128)(2,1)}, u32[]{:S(2)}, u32[]{:S(2)}) collective-permute-start(bf16[2,592,256]{2,1,0:T(8,128)(2,1)S(1)} %pad_maximum_fusion.refs_0_), channel_id=1, source_target_pairs={{0,32},{8,200},{16,48},{24,216},{32,64},{40,232},{48,80},{56,248},... | collective-permute-start | bytes 1818632 | tf_op jit(solution)/shard_map/ppermute | solution.py:204
  6.4 1.5 %collective-permute-start.1 = (bf16[1,592,256]{2,1,0:T(8,128)(2,1)}, bf16[1,592,256]{2,1,0:T(8,128)(2,1)S(1)}, u32[]{:S(2)}, u32[]{:S(2)}) collective-permute-start(bf16[1,592,256]{2,1,0:T(8,128)(2,1)} %maximum_bitcast_fusion), channel_id=1, source_target_pairs={{0,16},{8,24},{16,0},{24,8},{32,48},{40,56},{48,32},{56,40},{64,80... | collective-permute-start | bytes 909320 | tf_op jit(solution)/shard_map/ppermute | solution.py:197
  7.9 2.8 %copy.30 = bf16[1,256,4608]{1,2,0:T(8,128)(2,1)S(1)} copy(bf16[1,256,4608]{2,1,0:T(8,128)(2,1)} %param.5) | data formatting | bytes 4718592 | tf_op args[0]
  10.7 0.0 copy-done
  10.8 0.0 copy-done.1
  10.8 3.3 %attend.9 = (f32[8,256]{1,0:T(8,128)S(1)}, f32[8,256]{1,0:T(8,128)S(1)}, f32[8,512,256]{2,1,0:T(8,128)S(1)}) custom-call(s32[1,32]{1,0:T(1,128)S(1)} %constant_dynamic-slice_fusion.row, s32[1,256]{1,0:T(1,128)S(1)} %copy-done.1, s32[1,256]{1,0:T(1,128)S(1)} %copy-done.1, bf16[4608,256]{1,0:T(8,128)(2,1)S(1)} %bitcast.9, ...), custom_call_target="tpu_custom_call" | custom-call | flops 2281701376 | bytes 589824 | tf_op jit(solution)/shard_map/attend/pallas_call | solution.py:169
  14.1 1.9 %collective-permute-done.1.refs_0_ = bf16[1,592,256]{2,1,0:T(8,128)(2,1)S(1)} collective-permute-done((bf16[1,592,256]{2,1,0:T(8,128)(2,1)}, bf16[1,592,256]{2,1,0:T(8,128)(2,1)S(1)}, u32[]{:S(2)}, u32[]{:S(2)}) %collective-permute-start.1) | collective-permute-done | bytes 303136 | tf_op jit(solution)/shard_map/ppermute | solution.py:197
  16.0 0.1 collective-permute-start.4
  16.1 0.7 attend.10
  16.8 0.0 collective-permute-done.2.refs_1_
  16.8 1.1 %collective-permute-start.5 = (bf16[2,592,256]{2,1,0:T(8,128)(2,1)}, bf16[2,592,256]{2,1,0:T(8,128)(2,1)S(1)}, u32[]{:S(2)}, u32[]{:S(2)}) collective-permute-start(bf16[2,592,256]{2,1,0:T(8,128)(2,1)} %collective-permute-done.2.refs_1_), channel_id=1, source_target_pairs={{0,32},{8,232},{16,48},{24,248},{32,64},{40,8},{48,80},{56,24},{64... | collective-permute-start | bytes 1818632 | tf_op jit(solution)/shard_map/ppermute | solution.py:204
  17.9 4.9 %collective-permute-start.3 = (bf16[2,592,256]{2,1,0:T(8,128)(2,1)}, bf16[2,592,256]{2,1,0:T(8,128)(2,1)S(1)}, u32[]{:S(2)}, u32[]{:S(2)}) collective-permute-start(bf16[2,592,256]{2,1,0:T(8,128)(2,1)} %collective-permute-done.2.refs_1_), channel_id=1, source_target_pairs={{0,8},{8,0},{16,24},{24,16},{32,40},{40,32},{48,56},{56,48},{64,72... | collective-permute-start | bytes 1818632 | tf_op jit(solution)/shard_map/ppermute | solution.py:200
  22.7 1.9 %collective-permute-start.6 = (bf16[2,592,256]{2,1,0:T(8,128)(2,1)}, bf16[2,592,256]{2,1,0:T(8,128)(2,1)S(1)}, u32[]{:S(2)}, u32[]{:S(2)}) collective-permute-start(bf16[2,592,256]{2,1,0:T(8,128)(2,1)} %collective-permute-done.2.refs_1_), channel_id=1, source_target_pairs={{0,16},{8,24},{16,0},{24,8},{32,48},{40,56},{48,32},{56,40},{64,80... | collective-permute-start | bytes 1818632 | tf_op jit(solution)/shard_map/ppermute | solution.py:197
  24.6 0.0 collective-permute-done.4.refs_0_
  24.6 5.6 %attend.11 = (f32[8,256]{1,0:T(8,128)S(1)}, f32[8,256]{1,0:T(8,128)S(1)}, f32[8,512,256]{2,1,0:T(8,128)S(1)}) custom-call(s32[1,32]{1,0:T(1,128)S(1)} %constant_dynamic-slice_fusion.row, s32[1,256]{1,0:T(1,128)S(1)} %copy-done.1, s32[1,256]{1,0:T(1,128)S(1)} %copy-done.1, ...), custom_call_target="tpu_custom_call", output_to_operand_aliasing={{0}: (6, {}), {1}: (7, {}), {2}: (8, {})} | custom-call | flops 3422552064 | bytes 884736 | tf_op jit(solution)/shard_map/attend/pallas_call | solution.py:169
  30.3 0.0 collective-permute-done.5.refs_1_
  30.3 0.3 collective-permute-start.7
  30.5 1.6 %collective-permute-start.9 = (bf16[2,592,256]{2,1,0:T(8,128)(2,1)S(1)}, bf16[2,592,256]{2,1,0:T(8,128)(2,1)S(1)}, u32[]{:S(2)}, u32[]{:S(2)}) collective-permute-start(bf16[2,592,256]{2,1,0:T(8,128)(2,1)S(1)} %collective-permute-done.5.refs_1_), channel_id=1, source_target_pairs={{0,8},{8,0},{16,24},{24,16},{32,40},{40,32},{48,56},{56,48},{64,72... | collective-permute-start | bytes 1818632 | tf_op jit(solution)/shard_map/ppermute | solution.py:200
  32.2 0.0 collective-permute-done.3.refs_0_
  32.2 5.1 %attend.12 = (f32[8,256]{1,0:T(8,128)S(1)}, f32[8,256]{1,0:T(8,128)S(1)}, f32[8,512,256]{2,1,0:T(8,128)S(1)}) custom-call(s32[1,32]{1,0:T(1,128)S(1)} %constant_dynamic-slice_fusion.row, s32[1,256]{1,0:T(1,128)S(1)} %copy-done.1, s32[1,256]{1,0:T(1,128)S(1)} %copy-done.1, ...), custom_call_target="tpu_custom_call", output_to_operand_aliasing={{0}: (6, {}), {1}: (7, {}), {2}: (8, {})} | custom-call | flops 4563402752 | bytes 1179648 | tf_op jit(solution)/shard_map/attend/pallas_call | solution.py:169
  37.2 1.5 %collective-permute-done.6.refs_1_ = bf16[2,592,256]{2,1,0:T(8,128)(2,1)S(1)} collective-permute-done((bf16[2,592,256]{2,1,0:T(8,128)(2,1)}, bf16[2,592,256]{2,1,0:T(8,128)(2,1)S(1)}, u32[]{:S(2)}, u32[]{:S(2)}) %collective-permute-start.6) | collective-permute-done | bytes 606240 | tf_op jit(solution)/shard_map/ppermute | solution.py:197
  38.7 1.9 %collective-permute-done.7.refs_1_ = bf16[2,592,256]{2,1,0:T(8,128)(2,1)S(1)} collective-permute-done((bf16[2,592,256]{2,1,0:T(8,128)(2,1)S(1)}, bf16[2,592,256]{2,1,0:T(8,128)(2,1)S(1)}, u32[]{:S(2)}, u32[]{:S(2)}) %collective-permute-start.7) | collective-permute-done | bytes 606240 | tf_op jit(solution)/shard_map/ppermute | solution.py:204
  40.6 0.7 collective-permute-start.8
  41.3 3.0 %collective-permute-start.10 = (bf16[2,592,256]{2,1,0:T(8,128)(2,1)S(1)}, bf16[2,592,256]{2,1,0:T(8,128)(2,1)S(1)}, u32[]{:S(2)}, u32[]{:S(2)}) collective-permute-start(bf16[2,592,256]{2,1,0:T(8,128)(2,1)S(1)} %collective-permute-done.6.refs_1_), channel_id=1, source_target_pairs={{0,32},{8,232},{16,48},{24,248},{32,64},{40,8},{48,80},{56,24},{64... | collective-permute-start | bytes 1818632 | tf_op jit(solution)/shard_map/ppermute | solution.py:204
  44.3 0.5 collective-permute-start.11
  44.8 0.0 collective-permute-start.14
  44.8 0.0 collective-permute-done.9.refs_0_
  44.8 8.9 %attend.13 = (f32[8,256]{1,0:T(8,128)S(1)}, f32[8,256]{1,0:T(8,128)S(1)}, f32[8,512,256]{2,1,0:T(8,128)S(1)}) custom-call(s32[1,32]{1,0:T(1,128)S(1)} %constant_dynamic-slice_fusion.row, s32[1,256]{1,0:T(1,128)S(1)} %copy-done.1, s32[1,256]{1,0:T(1,128)S(1)} %copy-done.1, ...), custom_call_target="tpu_custom_call", output_to_operand_aliasing={{0}: (6, {}), {1}: (7, {}), {2}: (8, {})} | custom-call | flops 4563402752 | bytes 1179648 | tf_op jit(solution)/shard_map/attend/pallas_call | solution.py:169
  53.6 0.0 collective-permute-done.8.refs_0_
  53.6 5.1 %attend.14 = (f32[8,256]{1,0:T(8,128)S(1)}, f32[8,256]{1,0:T(8,128)S(1)}, f32[8,512,256]{2,1,0:T(8,128)S(1)}) custom-call(s32[1,32]{1,0:T(1,128)S(1)} %constant_dynamic-slice_fusion.row, s32[1,256]{1,0:T(1,128)S(1)} %copy-done.1, s32[1,256]{1,0:T(1,128)S(1)} %copy-done.1, ...), custom_call_target="tpu_custom_call", output_to_operand_aliasing={{0}: (6, {}), {1}: (7, {}), {2}: (8, {})} | custom-call | flops 4563402752 | bytes 1179648 | tf_op jit(solution)/shard_map/attend/pallas_call | solution.py:169
  58.7 0.0 collective-permute-done.10.refs_0_
  58.7 0.0 collective-permute-done.11.refs_2_
  58.7 0.0 copy-start.2
  58.7 2.5 %collective-permute-start.12 = (bf16[2,592,256]{2,1,0:T(8,128)(2,1)S(1)}, bf16[2,592,256]{2,1,0:T(8,128)(2,1)S(1)}, u32[]{:S(2)}, u32[]{:S(2)}) collective-permute-start(bf16[2,592,256]{2,1,0:T(8,128)(2,1)S(1)} %collective-permute-done.10.refs_0_), channel_id=1, source_target_pairs={{0,8},{8,0},{16,24},{24,16},{32,40},{40,32},{48,56},{56,48},{64,72... | collective-permute-start | bytes 1818632 | tf_op jit(solution)/shard_map/ppermute | solution.py:200
  61.3 0.1 collective-permute-start.13
  61.4 0.0 collective-permute-done.14.refs_0_
  61.4 5.2 %attend.15 = (f32[8,256]{1,0:T(8,128)S(1)}, f32[8,256]{1,0:T(8,128)S(1)}, f32[8,512,256]{2,1,0:T(8,128)S(1)}) custom-call(s32[1,32]{1,0:T(1,128)S(1)} %constant_dynamic-slice_fusion.row, s32[1,256]{1,0:T(1,128)S(1)} %copy-done.1, s32[1,256]{1,0:T(1,128)S(1)} %copy-done.1, ...), custom_call_target="tpu_custom_call", output_to_operand_aliasing={{0}: (5, {}), {1}: (6, {}), {2}: (7, {})} | custom-call | flops 2281701376 | bytes 589824 | tf_op jit(solution)/shard_map/attend/pallas_call | solution.py:169
  66.6 0.0 collective-permute-done.12.refs_1_
  66.6 0.0 collective-permute-done.13.refs_3_
  66.6 0.0 copy-done.2
  66.6 10.9 %attend.16 = (f32[8,256]{1,0:T(8,128)S(1)}, f32[8,256]{1,0:T(8,128)S(1)}, f32[8,512,256]{2,1,0:T(8,128)S(1)}, bf16[256,768]{1,0:T(8,128)(2,1)S(1)}) custom-call(s32[1,32]{1,0:T(1,128)S(1)} %constant_dynamic-slice_fusion.row, s32[1,256]{1,0:T(1,128)S(1)} %copy-done.1, ...), custom_call_target="tpu_custom_call", output_to_operand_aliasing={{0}: (9, {}), {1}: (10, {}), {2}: (11, {})} | custom-call | flops 9126805504 | bytes 2359296 | tf_op jit(solution)/shard_map/attend/pallas_call | solution.py:169
  77.5 4.7 %collective-permute-start.15 = (bf16[1,256,768]{2,1,0:T(8,128)(2,1)S(1)}, bf16[1,256,768]{2,1,0:T(8,128)(2,1)S(1)}, u32[]{:S(2)}, u32[]{:S(2)}) collective-permute-start(bf16[1,256,768]{2,1,0:T(8,128)(2,1)S(1)} %bitcast.20), channel_id=1, source_target_pairs={{0,1},{1,2},{2,3},{3,4},{4,5},{5,6},{6,7},{7,0},{8,9},{9,10},{10,1... | collective-permute-start | bytes 1179656 | tf_op jit(solution)/shard_map/ppermute | solution.py:241
  82.3 5.3 %attend.17 = (f32[8,256]{1,0:T(8,128)S(1)}, f32[8,256]{1,0:T(8,128)S(1)}, f32[8,512,256]{2,1,0:T(8,128)S(1)}, bf16[256,256]{1,0:T(8,128)(2,1)S(1)}) custom-call(s32[1,32]{1,0:T(1,128)S(1)} %constant_dynamic-slice_fusion.row, s32[1,256]{1,0:T(1,128)S(1)} %copy-done.1, ...), custom_call_target="tpu_custom_call", output_to_operand_aliasing={{0}: (9, {}), {1}: (10, {}), {2}: (11, {})} | custom-call | flops 9126805504 | bytes 2359296 | tf_op jit(solution)/shard_map/attend/pallas_call | solution.py:169
  87.6 0.1 collective-permute-start.16
  87.7 8.6 %collective-permute-done.16 = bf16[1,256,256]{2,1,0:T(8,128)(2,1)S(1)} collective-permute-done((bf16[1,256,256]{2,1,0:T(8,128)(2,1)S(1)}, bf16[1,256,256]{2,1,0:T(8,128)(2,1)S(1)}, u32[]{:S(2)}, u32[]{:S(2)}) %collective-permute-start.16) | collective-permute-done | bytes 131104 | tf_op jit(solution)/shard_map/ppermute | solution.py:241
  96.3 0.0 collective-permute-done.15
  96.3 0.9 pad_maximum_fusion.1
  (2 shorter events, 0.0 us)
Async XLA Ops:
  0.0 10.7 %copy-start = (s32[32,32]{1,0:T(8,128)S(1)}, s32[32,32]{1,0:T(8,128)}, u32[]{:S(2)}) copy-start(s32[32,32]{1,0:T(8,128)} %param.8) | copy-start | bytes 12292
  0.0 10.8 %copy-start.1 = (s32[1,256]{1,0:T(1,128)S(1)}, s32[1,256]{1,0:T(1,128)}, u32[]{:S(2)}) copy-start(s32[1,256]{1,0:T(1,128)} %ids_v.17) | copy-start | bytes 3076
  2.5 1.8 %collective-permute-start = (bf16[1,592,256]{2,1,0:T(8,128)(2,1)}, bf16[1,592,256]{2,1,0:T(8,128)(2,1)S(1)}, u32[]{:S(2)}, u32[]{:S(2)}) collective-permute-start(bf16[1,592,256]{2,1,0:T(8,128)(2,1)} %maximum_bitcast_fusion), channel_id=1, source_target_pairs={{0,8},{8,0},{16,24},{24,16},{32,40},{40,32},{48,56},{56,48},{64,72... | collective-permute-start | bytes 909320 | tf_op jit(solution)/shard_map/ppermute | solution.py:200
  5.3 11.4 %collective-permute-start.2 = (bf16[2,592,256]{2,1,0:T(8,128)(2,1)S(1)}, bf16[2,592,256]{2,1,0:T(8,128)(2,1)}, u32[]{:S(2)}, u32[]{:S(2)}) collective-permute-start(bf16[2,592,256]{2,1,0:T(8,128)(2,1)S(1)} %pad_maximum_fusion.refs_0_), channel_id=1, source_target_pairs={{0,32},{8,200},{16,48},{24,216},{32,64},{40,232},{48,80},{56,248},... | collective-permute-start | bytes 1818632 | tf_op jit(solution)/shard_map/ppermute | solution.py:204
  6.4 9.6 %collective-permute-start.1 = (bf16[1,592,256]{2,1,0:T(8,128)(2,1)}, bf16[1,592,256]{2,1,0:T(8,128)(2,1)S(1)}, u32[]{:S(2)}, u32[]{:S(2)}) collective-permute-start(bf16[1,592,256]{2,1,0:T(8,128)(2,1)} %maximum_bitcast_fusion), channel_id=1, source_target_pairs={{0,16},{8,24},{16,0},{24,8},{32,48},{40,56},{48,32},{56,40},{64,80... | collective-permute-start | bytes 909320 | tf_op jit(solution)/shard_map/ppermute | solution.py:197
  16.0 8.6 %collective-permute-start.4 = (bf16[1,592,256]{2,1,0:T(8,128)(2,1)S(1)}, bf16[1,592,256]{2,1,0:T(8,128)(2,1)S(1)}, u32[]{:S(2)}, u32[]{:S(2)}) collective-permute-start(bf16[1,592,256]{2,1,0:T(8,128)(2,1)S(1)} %collective-permute-done.1.refs_0_), channel_id=1, source_target_pairs={{0,8},{8,0},{16,24},{24,16},{32,40},{40,32},{48,56},{56,48},{64,72... | collective-permute-start | bytes 909320 | tf_op jit(solution)/shard_map/ppermute | solution.py:200
  16.8 13.5 %collective-permute-start.5 = (bf16[2,592,256]{2,1,0:T(8,128)(2,1)}, bf16[2,592,256]{2,1,0:T(8,128)(2,1)S(1)}, u32[]{:S(2)}, u32[]{:S(2)}) collective-permute-start(bf16[2,592,256]{2,1,0:T(8,128)(2,1)} %collective-permute-done.2.refs_1_), channel_id=1, source_target_pairs={{0,32},{8,232},{16,48},{24,248},{32,64},{40,8},{48,80},{56,24},{64... | collective-permute-start | bytes 1818632 | tf_op jit(solution)/shard_map/ppermute | solution.py:204
  17.9 14.3 %collective-permute-start.3 = (bf16[2,592,256]{2,1,0:T(8,128)(2,1)}, bf16[2,592,256]{2,1,0:T(8,128)(2,1)S(1)}, u32[]{:S(2)}, u32[]{:S(2)}) collective-permute-start(bf16[2,592,256]{2,1,0:T(8,128)(2,1)} %collective-permute-done.2.refs_1_), channel_id=1, source_target_pairs={{0,8},{8,0},{16,24},{24,16},{32,40},{40,32},{48,56},{56,48},{64,72... | collective-permute-start | bytes 1818632 | tf_op jit(solution)/shard_map/ppermute | solution.py:200
  22.7 16.0 %collective-permute-start.6 = (bf16[2,592,256]{2,1,0:T(8,128)(2,1)}, bf16[2,592,256]{2,1,0:T(8,128)(2,1)S(1)}, u32[]{:S(2)}, u32[]{:S(2)}) collective-permute-start(bf16[2,592,256]{2,1,0:T(8,128)(2,1)} %collective-permute-done.2.refs_1_), channel_id=1, source_target_pairs={{0,16},{8,24},{16,0},{24,8},{32,48},{40,56},{48,32},{56,40},{64,80... | collective-permute-start | bytes 1818632 | tf_op jit(solution)/shard_map/ppermute | solution.py:197
  30.3 10.3 %collective-permute-start.7 = (bf16[2,592,256]{2,1,0:T(8,128)(2,1)S(1)}, bf16[2,592,256]{2,1,0:T(8,128)(2,1)S(1)}, u32[]{:S(2)}, u32[]{:S(2)}) collective-permute-start(bf16[2,592,256]{2,1,0:T(8,128)(2,1)S(1)} %collective-permute-done.5.refs_1_), channel_id=1, source_target_pairs={{0,32},{8,232},{16,48},{24,248},{32,64},{40,8},{48,80},{56,24},{64... | collective-permute-start | bytes 1818632 | tf_op jit(solution)/shard_map/ppermute | solution.py:204
  30.5 14.2 %collective-permute-start.9 = (bf16[2,592,256]{2,1,0:T(8,128)(2,1)S(1)}, bf16[2,592,256]{2,1,0:T(8,128)(2,1)S(1)}, u32[]{:S(2)}, u32[]{:S(2)}) collective-permute-start(bf16[2,592,256]{2,1,0:T(8,128)(2,1)S(1)} %collective-permute-done.5.refs_1_), channel_id=1, source_target_pairs={{0,8},{8,0},{16,24},{24,16},{32,40},{40,32},{48,56},{56,48},{64,72... | collective-permute-start | bytes 1818632 | tf_op jit(solution)/shard_map/ppermute | solution.py:200
  40.6 13.0 %collective-permute-start.8 = (bf16[2,592,256]{2,1,0:T(8,128)(2,1)S(1)}, bf16[2,592,256]{2,1,0:T(8,128)(2,1)S(1)}, u32[]{:S(2)}, u32[]{:S(2)}) collective-permute-start(bf16[2,592,256]{2,1,0:T(8,128)(2,1)S(1)} %collective-permute-done.6.refs_1_), channel_id=1, source_target_pairs={{0,8},{8,0},{16,24},{24,16},{32,40},{40,32},{48,56},{56,48},{64,72... | collective-permute-start | bytes 1818632 | tf_op jit(solution)/shard_map/ppermute | solution.py:200
  41.3 17.4 %collective-permute-start.10 = (bf16[2,592,256]{2,1,0:T(8,128)(2,1)S(1)}, bf16[2,592,256]{2,1,0:T(8,128)(2,1)S(1)}, u32[]{:S(2)}, u32[]{:S(2)}) collective-permute-start(bf16[2,592,256]{2,1,0:T(8,128)(2,1)S(1)} %collective-permute-done.6.refs_1_), channel_id=1, source_target_pairs={{0,32},{8,232},{16,48},{24,248},{32,64},{40,8},{48,80},{56,24},{64... | collective-permute-start | bytes 1818632 | tf_op jit(solution)/shard_map/ppermute | solution.py:204
  44.3 14.5 %collective-permute-start.11 = (bf16[2,592,256]{2,1,0:T(8,128)(2,1)S(1)}, bf16[2,592,256]{2,1,0:T(8,128)(2,1)S(1)}, u32[]{:S(2)}, u32[]{:S(2)}) collective-permute-start(bf16[2,592,256]{2,1,0:T(8,128)(2,1)S(1)} %collective-permute-done.7.refs_1_), channel_id=1, source_target_pairs={{0,16},{8,24},{16,0},{24,8},{32,48},{40,56},{48,32},{56,40},{64,80... | collective-permute-start | bytes 1818632 | tf_op jit(solution)/shard_map/ppermute | solution.py:197
  44.8 16.6 %collective-permute-start.14 = (bf16[2,592,256]{2,1,0:T(8,128)(2,1)S(1)}, bf16[2,592,256]{2,1,0:T(8,128)(2,1)S(1)}, u32[]{:S(2)}, u32[]{:S(2)}) collective-permute-start(bf16[2,592,256]{2,1,0:T(8,128)(2,1)S(1)} %collective-permute-done.7.refs_1_), channel_id=1, source_target_pairs={{0,8},{8,0},{16,24},{24,16},{32,40},{40,32},{48,56},{56,48},{64,72... | collective-permute-start | bytes 1818632 | tf_op jit(solution)/shard_map/ppermute | solution.py:200
  58.7 7.9 %copy-start.2 = (bf16[1,8,512,128]{3,2,1,0:T(8,128)(2,1)S(1)}, bf16[1,8,512,128]{3,2,1,0:T(8,128)(2,1)}, u32[]{:S(2)}) copy-start(bf16[1,8,512,128]{3,2,1,0:T(8,128)(2,1)} %param.9) | copy-start | bytes 3145732
  58.7 7.9 %collective-permute-start.12 = (bf16[2,592,256]{2,1,0:T(8,128)(2,1)S(1)}, bf16[2,592,256]{2,1,0:T(8,128)(2,1)S(1)}, u32[]{:S(2)}, u32[]{:S(2)}) collective-permute-start(bf16[2,592,256]{2,1,0:T(8,128)(2,1)S(1)} %collective-permute-done.10.refs_0_), channel_id=1, source_target_pairs={{0,8},{8,0},{16,24},{24,16},{32,40},{40,32},{48,56},{56,48},{64,72... | collective-permute-start | bytes 1818632 | tf_op jit(solution)/shard_map/ppermute | solution.py:200
  61.3 5.4 %collective-permute-start.13 = (bf16[2,592,256]{2,1,0:T(8,128)(2,1)S(1)}, bf16[2,592,256]{2,1,0:T(8,128)(2,1)S(1)}, u32[]{:S(2)}, u32[]{:S(2)}) collective-permute-start(bf16[2,592,256]{2,1,0:T(8,128)(2,1)S(1)} %collective-permute-done.11.refs_2_), channel_id=1, source_target_pairs={{0,8},{8,0},{16,24},{24,16},{32,40},{40,32},{48,56},{56,48},{64,72... | collective-permute-start | bytes 1818632 | tf_op jit(solution)/shard_map/ppermute | solution.py:200
  77.5 18.7 %collective-permute-start.15 = (bf16[1,256,768]{2,1,0:T(8,128)(2,1)S(1)}, bf16[1,256,768]{2,1,0:T(8,128)(2,1)S(1)}, u32[]{:S(2)}, u32[]{:S(2)}) collective-permute-start(bf16[1,256,768]{2,1,0:T(8,128)(2,1)S(1)} %bitcast.20), channel_id=1, source_target_pairs={{0,1},{1,2},{2,3},{3,4},{4,5},{5,6},{6,7},{7,0},{8,9},{9,10},{10,1... | collective-permute-start | bytes 1179656 | tf_op jit(solution)/shard_map/ppermute | solution.py:241
  87.6 8.7 %collective-permute-start.16 = (bf16[1,256,256]{2,1,0:T(8,128)(2,1)S(1)}, bf16[1,256,256]{2,1,0:T(8,128)(2,1)S(1)}, u32[]{:S(2)}, u32[]{:S(2)}) collective-permute-start(bf16[1,256,256]{2,1,0:T(8,128)(2,1)S(1)} %bitcast.21), channel_id=1, source_target_pairs={{0,1},{1,2},{2,3},{3,4},{4,5},{5,6},{6,7},{7,0},{8,9},{9,10},{10,1... | collective-permute-start | bytes 393224 | tf_op jit(solution)/shard_map/ppermute | solution.py:241
where the time goes:
time: 97.9 us; the launch traced here: 97.1 us
  Pallas kernels  50 us (51%)
  starting transfers between devices  24 us (25%)
  waiting for transfers between devices  15.7 us (16%)
  other arithmetic  4.34 us (4%)
  local copies, waits for them, and re-layouts  2.86 us (3%)
    pallas_call x9, Pallas kernels, stage(): pl.pallas_call(functools.partial(attend, tuple(places), first, chosen, fi...  50 us
    ppermute x8, starting transfers between devices, core(): return lax.ppermute(x, 'ctx', [(i, i ^ 1) for i in range(devices)])  9.92 us
    ppermute x2, waiting for transfers between devices, shards(): lax.ppermute(heads_out[None], 'section', [(i, (i + 1) % sections) for i i...  8.57 us
    ppermute x4, starting transfers between devices, along(): lax.ppermute(x, 'ctx', [(i, (i + 4 if i % 2 == 0 else i - down) % devices...  5.4 us
    ppermute x2, starting transfers between devices, shards(): lax.ppermute(heads_out[None], 'section', [(i, (i + 1) % sections) for i i...  4.8 us
    ppermute x3, starting transfers between devices, across(): return lax.ppermute(x, 'ctx', [(i, i ^ 2) for i in range(devices)])  3.87 us
    ppermute x3, waiting for transfers between devices, across(): return lax.ppermute(x, 'ctx', [(i, i ^ 2) for i in range(devices)])  3.43 us
    unnamed x7, local copies, waits for them, and re-layouts  2.84 us
  transfers between devices with their start and end apart: 17, of which 5 were waited for; matrix products, arithmetic and copies ran while one was open for 3% of the time, Pallas kernels for 40%

commit v1 on v0

--- a/solution.py
+++ b/solution.py
@@ -227,16 +227,15 @@
     state = run([(1, 0, 1), (2, 0, 0)], [cz1, z2], state)
     *state, x1, z3 = tie(*state, x1, z3)
     x3, xz2, cx1, cz3 = across(z3), along(x1, 2), core(x1), core(z3)
-    state = run([(2, 0, 1), (1, 1, 0)], [cz2, x1], state)
-    state = run([(1, 1, 1), (3, 0, 0)], [cx1, z3], state)
+    state = run([(2, 0, 1), (1, 1, 0), (3, 0, 0)], [cz2, x1, z3], state)
     *state, xz2, x3 = tie(*state, xz2, x3)
     cxz2, cx3 = core(xz2), core(x3)
-    state = run([(3, 0, 1)], [cz3], state)
+    state = run([(1, 1, 1), (3, 0, 1), (2, 1, 0)], [cx1, cz3, xz2], state)
     sections = lax.axis_size("section")
     handed = []
     for part in (tuple(range(heads - heads // 4)), tuple(range(heads - heads // 4, heads))):
         *state, heads_out = run(
-            [(2, 1, 0), (2, 1, 1), (3, 1, 0), (3, 1, 1)], [xz2, cxz2, x3, cx3], state, w_uv[0], part
+            [(2, 1, 1), (3, 1, 0), (3, 1, 1)], [cxz2, x3, cx3], state, w_uv[0], part
         )
         handed.append(lax.ppermute(heads_out[None], "section", [(i, (i + 1) % sections) for i in range(sections)]))
     return jnp.concatenate(handed, axis=2)

time: 97.9 us -> 98.5 us (level)
  the two profiles are of different devices: /device:TPU:192 before, /device:TPU:224 now
where the time goes in v1:
time: 98.5 us; the launch traced here: 99.2 us
  Pallas kernels  53.4 us (54%)
  waiting for transfers between devices  19.9 us (20%)
  starting transfers between devices  18.5 us (19%)
  other arithmetic  4.34 us (4%)
  local copies, waits for them, and re-layouts  2.86 us (3%)
    pallas_call x8, Pallas kernels, stage(): pl.pallas_call(functools.partial(attend, tuple(places), first, chosen, fi...  53.4 us
    ppermute x2, waiting for transfers between devices, shards(): lax.ppermute(heads_out[None], 'section', [(i, (i + 1) % sections) for i i...  8.56 us
    ppermute x3, waiting for transfers between devices, across(): return lax.ppermute(x, 'ctx', [(i, i ^ 2) for i in range(devices)])  7.6 us
    ppermute x8, starting transfers between devices, core(): return lax.ppermute(x, 'ctx', [(i, i ^ 1) for i in range(devices)])  7.26 us
    ppermute x3, starting transfers between devices, across(): return lax.ppermute(x, 'ctx', [(i, i ^ 2) for i in range(devices)])  4.63 us
    ppermute x4, starting transfers between devices, along(): lax.ppermute(x, 'ctx', [(i, (i + 4 if i % 2 == 0 else i - down) % devices...  3.86 us
    unnamed x7, local copies, waits for them, and re-layouts  2.84 us
    ppermute x2, starting transfers between devices, shards(): lax.ppermute(heads_out[None], 'section', [(i, (i + 1) % sections) for i i...  2.72 us
  transfers between devices with their start and end apart: 17, of which 6 were waited for; matrix products, arithmetic and copies ran while one was open for 3% of the time, Pallas kernels for 43%

profile of v1, /device:TPU:224, one launch (start us, length us, event | category | flops | bytes accessed | tf_op | source)
XLA Modules:
  0.0 99.2 jit_solution(12322605112839676958)
XLA Ops:
  0.0 0.0 copy-start
  0.0 0.0 copy-start.1
  0.0 0.8 convert_reduce_fusion
  0.8 1.7 %maximum_bitcast_fusion = bf16[1,592,256]{2,1,0:T(8,128)(2,1)} fusion(bf16[16,256]{1,0:T(8,128)(2,1)S(1)} %broadcast_in_dim.17, bf16[576,256]{1,0:T(8,128)(2,1)} %bitcast.21), kind=kLoop, calls=%fused_computation.2 | loop fusion | flops 606208 | bytes 606208 | tf_op jit(solution)/shard_map/broadcast_in_dim | solution.py:207
  2.5 0.0 collective-permute-start
  2.5 1.8 %collective-permute-done = bf16[1,592,256]{2,1,0:T(8,128)(2,1)S(1)} collective-permute-done((bf16[1,592,256]{2,1,0:T(8,128)(2,1)}, bf16[1,592,256]{2,1,0:T(8,128)(2,1)S(1)}, u32[]{:S(2)}, u32[]{:S(2)}) %collective-permute-start) | collective-permute-done | bytes 303136 | tf_op jit(solution)/shard_map/ppermute | solution.py:200
  4.3 1.0 %pad_maximum_fusion.refs_0_ = bf16[2,592,256]{2,1,0:T(8,128)(2,1)S(1)} fusion(bf16[1,592,256]{2,1,0:T(8,128)(2,1)S(1)} %collective-permute-done, bf16[1,592,256]{2,1,0:T(8,128)(2,1)} %maximum_bitcast_fusion), kind=kLoop, calls=%fused_computation | loop fusion | flops 303104 | bytes 1212416 | tf_op jit(solution)/shard_map/concatenate | solution.py:211
  5.3 0.1 collective-permute-start.3
  5.4 1.6 %collective-permute-start.1 = (bf16[1,592,256]{2,1,0:T(8,128)(2,1)}, bf16[1,592,256]{2,1,0:T(8,128)(2,1)S(1)}, u32[]{:S(2)}, u32[]{:S(2)}) collective-permute-start(bf16[1,592,256]{2,1,0:T(8,128)(2,1)} %maximum_bitcast_fusion), channel_id=1, source_target_pairs={{0,16},{8,24},{16,0},{24,8},{32,48},{40,56},{48,32},{56,40},{64,80... | collective-permute-start | bytes 909320 | tf_op jit(solution)/shard_map/ppermute | solution.py:197
  7.0 2.8 %copy.27 = bf16[1,256,4608]{1,2,0:T(8,128)(2,1)S(1)} copy(bf16[1,256,4608]{2,1,0:T(8,128)(2,1)} %param.5) | data formatting | bytes 4718592 | tf_op args[0]
  9.8 0.0 copy-done
  9.8 0.0 copy-done.1
  9.9 3.3 %attend.8 = (f32[8,256]{1,0:T(8,128)S(1)}, f32[8,256]{1,0:T(8,128)S(1)}, f32[8,512,256]{2,1,0:T(8,128)S(1)}) custom-call(s32[1,32]{1,0:T(1,128)S(1)} %constant_dynamic-slice_fusion.row, s32[1,256]{1,0:T(1,128)S(1)} %copy-done.1, s32[1,256]{1,0:T(1,128)S(1)} %copy-done.1, bf16[4608,256]{1,0:T(8,128)(2,1)S(1)} %bitcast.9, ...), custom_call_target="tpu_custom_call" | custom-call | flops 2281701376 | bytes 589824 | tf_op jit(solution)/shard_map/attend/pallas_call | solution.py:169
  13.2 2.3 %collective-permute-done.1.refs_0_ = bf16[1,592,256]{2,1,0:T(8,128)(2,1)S(1)} collective-permute-done((bf16[1,592,256]{2,1,0:T(8,128)(2,1)}, bf16[1,592,256]{2,1,0:T(8,128)(2,1)S(1)}, u32[]{:S(2)}, u32[]{:S(2)}) %collective-permute-start.1) | collective-permute-done | bytes 303136 | tf_op jit(solution)/shard_map/ppermute | solution.py:197
  15.5 0.6 collective-permute-start.2
  16.2 0.7 attend.9
  16.8 0.0 collective-permute-done.3.refs_1_
  16.9 2.3 %collective-permute-start.4 = (bf16[2,592,256]{2,1,0:T(8,128)(2,1)}, bf16[2,592,256]{2,1,0:T(8,128)(2,1)S(1)}, u32[]{:S(2)}, u32[]{:S(2)}) collective-permute-start(bf16[2,592,256]{2,1,0:T(8,128)(2,1)} %collective-permute-done.3.refs_1_), channel_id=1, source_target_pairs={{0,32},{8,232},{16,48},{24,248},{32,64},{40,8},{48,80},{56,24},{64... | collective-permute-start | bytes 1818632 | tf_op jit(solution)/shard_map/ppermute | solution.py:204
  19.2 3.6 %collective-permute-start.6 = (bf16[2,592,256]{2,1,0:T(8,128)(2,1)}, bf16[2,592,256]{2,1,0:T(8,128)(2,1)S(1)}, u32[]{:S(2)}, u32[]{:S(2)}) collective-permute-start(bf16[2,592,256]{2,1,0:T(8,128)(2,1)} %collective-permute-done.3.refs_1_), channel_id=1, source_target_pairs={{0,8},{8,0},{16,24},{24,16},{32,40},{40,32},{48,56},{56,48},{64,72... | collective-permute-start | bytes 1818632 | tf_op jit(solution)/shard_map/ppermute | solution.py:200
  22.8 2.6 %collective-permute-start.7 = (bf16[2,592,256]{2,1,0:T(8,128)(2,1)}, bf16[2,592,256]{2,1,0:T(8,128)(2,1)S(1)}, u32[]{:S(2)}, u32[]{:S(2)}) collective-permute-start(bf16[2,592,256]{2,1,0:T(8,128)(2,1)} %collective-permute-done.3.refs_1_), channel_id=1, source_target_pairs={{0,16},{8,24},{16,0},{24,8},{32,48},{40,56},{48,32},{56,40},{64,80... | collective-permute-start | bytes 1818632 | tf_op jit(solution)/shard_map/ppermute | solution.py:197
  25.4 0.0 collective-permute-done.2.refs_0_
  25.4 5.7 %attend.10 = (f32[8,256]{1,0:T(8,128)S(1)}, f32[8,256]{1,0:T(8,128)S(1)}, f32[8,512,256]{2,1,0:T(8,128)S(1)}) custom-call(s32[1,32]{1,0:T(1,128)S(1)} %constant_dynamic-slice_fusion.row, s32[1,256]{1,0:T(1,128)S(1)} %copy-done.1, s32[1,256]{1,0:T(1,128)S(1)} %copy-done.1, ...), custom_call_target="tpu_custom_call", output_to_operand_aliasing={{0}: (6, {}), {1}: (7, {}), {2}: (8, {})} | custom-call | flops 3422552064 | bytes 884736 | tf_op jit(solution)/shard_map/attend/pallas_call | solution.py:169
  31.0 0.0 collective-permute-done.4.refs_1_
  31.1 0.3 collective-permute-start.8
  31.3 1.8 %collective-permute-start.5 = (bf16[2,592,256]{2,1,0:T(8,128)(2,1)S(1)}, bf16[2,592,256]{2,1,0:T(8,128)(2,1)S(1)}, u32[]{:S(2)}, u32[]{:S(2)}) collective-permute-start(bf16[2,592,256]{2,1,0:T(8,128)(2,1)S(1)} %collective-permute-done.4.refs_1_), channel_id=1, source_target_pairs={{0,8},{8,0},{16,24},{24,16},{32,40},{40,32},{48,56},{56,48},{64,72... | collective-permute-start | bytes 1818632 | tf_op jit(solution)/shard_map/ppermute | solution.py:200
  33.1 0.0 collective-permute-done.6.refs_0_
  33.1 5.1 %attend.11 = (f32[8,256]{1,0:T(8,128)S(1)}, f32[8,256]{1,0:T(8,128)S(1)}, f32[8,512,256]{2,1,0:T(8,128)S(1)}) custom-call(s32[1,32]{1,0:T(1,128)S(1)} %constant_dynamic-slice_fusion.row, s32[1,256]{1,0:T(1,128)S(1)} %copy-done.1, s32[1,256]{1,0:T(1,128)S(1)} %copy-done.1, ...), custom_call_target="tpu_custom_call", output_to_operand_aliasing={{0}: (6, {}), {1}: (7, {}), {2}: (8, {})} | custom-call | flops 4563402752 | bytes 1179648 | tf_op jit(solution)/shard_map/attend/pallas_call | solution.py:169
  38.3 1.2 %collective-permute-done.7.refs_1_ = bf16[2,592,256]{2,1,0:T(8,128)(2,1)S(1)} collective-permute-done((bf16[2,592,256]{2,1,0:T(8,128)(2,1)}, bf16[2,592,256]{2,1,0:T(8,128)(2,1)S(1)}, u32[]{:S(2)}, u32[]{:S(2)}) %collective-permute-start.7) | collective-permute-done | bytes 606240 | tf_op jit(solution)/shard_map/ppermute | solution.py:197
  39.4 1.9 %collective-permute-done.8.refs_2_ = bf16[2,592,256]{2,1,0:T(8,128)(2,1)S(1)} collective-permute-done((bf16[2,592,256]{2,1,0:T(8,128)(2,1)S(1)}, bf16[2,592,256]{2,1,0:T(8,128)(2,1)S(1)}, u32[]{:S(2)}, u32[]{:S(2)}) %collective-permute-start.8) | collective-permute-done | bytes 606240 | tf_op jit(solution)/shard_map/ppermute | solution.py:204
  41.4 1.2 %collective-permute-start.9 = (bf16[2,592,256]{2,1,0:T(8,128)(2,1)S(1)}, bf16[2,592,256]{2,1,0:T(8,128)(2,1)S(1)}, u32[]{:S(2)}, u32[]{:S(2)}) collective-permute-start(bf16[2,592,256]{2,1,0:T(8,128)(2,1)S(1)} %collective-permute-done.7.refs_1_), channel_id=1, source_target_pairs={{0,32},{8,232},{16,48},{24,248},{32,64},{40,8},{48,80},{56,24},{64... | collective-permute-start | bytes 1818632 | tf_op jit(solution)/shard_map/ppermute | solution.py:204
  42.6 0.7 collective-permute-start.13
  43.2 0.5 collective-permute-start.10
  43.7 0.0 collective-permute-start.14
  43.7 0.0 collective-permute-done.5.refs_0_
  43.7 11.0 %attend.12 = (f32[8,256]{1,0:T(8,128)S(1)}, f32[8,256]{1,0:T(8,128)S(1)}, f32[8,512,256]{2,1,0:T(8,128)S(1)}) custom-call(s32[1,32]{1,0:T(1,128)S(1)} %constant_dynamic-slice_fusion.row, s32[1,256]{1,0:T(1,128)S(1)} %copy-done.1, s32[1,256]{1,0:T(1,128)S(1)} %copy-done.1, ...), custom_call_target="tpu_custom_call", output_to_operand_aliasing={{0}: (7, {}), {1}: (8, {}), {2}: (9, {})} | custom-call | flops 6845104128 | bytes 1769472 | tf_op jit(solution)/shard_map/attend/pallas_call | solution.py:169
  54.7 4.1 %collective-permute-done.10.refs_1_ = bf16[2,592,256]{2,1,0:T(8,128)(2,1)S(1)} collective-permute-done((bf16[2,592,256]{2,1,0:T(8,128)(2,1)S(1)}, bf16[2,592,256]{2,1,0:T(8,128)(2,1)S(1)}, u32[]{:S(2)}, u32[]{:S(2)}) %collective-permute-start.10) | collective-permute-done | bytes 606240 | tf_op jit(solution)/shard_map/ppermute | solution.py:197
  58.8 0.0 collective-permute-done.9.refs_2_
  58.8 0.0 copy-start.2
  58.8 0.0 collective-permute-start.11
  58.8 0.5 collective-permute-start.12
  59.4 0.0 collective-permute-done.13.refs_0_
  59.4 0.0 collective-permute-done.14.refs_1_
  59.4 11.0 %attend.13 = (f32[8,256]{1,0:T(8,128)S(1)}, f32[8,256]{1,0:T(8,128)S(1)}, f32[8,512,256]{2,1,0:T(8,128)S(1)}) custom-call(s32[1,32]{1,0:T(1,128)S(1)} %constant_dynamic-slice_fusion.row, s32[1,256]{1,0:T(1,128)S(1)} %copy-done.1, s32[1,256]{1,0:T(1,128)S(1)} %copy-done.1, ...), custom_call_target="tpu_custom_call", output_to_operand_aliasing={{0}: (7, {}), {1}: (8, {}), {2}: (9, {})} | custom-call | flops 6845104128 | bytes 1769472 | tf_op jit(solution)/shard_map/attend/pallas_call | solution.py:169
  70.4 0.0 collective-permute-done.11.refs_0_
  70.4 0.0 collective-permute-done.12.refs_2_
  70.4 0.0 copy-done.2
  70.4 11.3 %attend.14 = (f32[8,256]{1,0:T(8,128)S(1)}, f32[8,256]{1,0:T(8,128)S(1)}, f32[8,512,256]{2,1,0:T(8,128)S(1)}, bf16[256,768]{1,0:T(8,128)(2,1)S(1)}) custom-call(s32[1,32]{1,0:T(1,128)S(1)} %constant_dynamic-slice_fusion.row, s32[1,256]{1,0:T(1,128)S(1)} %copy-done.1, ...), custom_call_target="tpu_custom_call", output_to_operand_aliasing={{0}: (8, {}), {1}: (9, {}), {2}: (10, {})} | custom-call | flops 6845104128 | bytes 1769472 | tf_op jit(solution)/shard_map/attend/pallas_call | solution.py:169
  81.7 2.6 %collective-permute-start.15 = (bf16[1,256,768]{2,1,0:T(8,128)(2,1)S(1)}, bf16[1,256,768]{2,1,0:T(8,128)(2,1)S(1)}, u32[]{:S(2)}, u32[]{:S(2)}) collective-permute-start(bf16[1,256,768]{2,1,0:T(8,128)(2,1)S(1)} %bitcast.19), channel_id=1, source_target_pairs={{0,1},{1,2},{2,3},{3,4},{4,5},{5,6},{6,7},{7,0},{8,9},{9,10},{10,1... | collective-permute-start | bytes 1179656 | tf_op jit(solution)/shard_map/ppermute | solution.py:240
  84.3 5.4 %attend.15 = (f32[8,256]{1,0:T(8,128)S(1)}, f32[8,256]{1,0:T(8,128)S(1)}, f32[8,512,256]{2,1,0:T(8,128)S(1)}, bf16[256,256]{1,0:T(8,128)(2,1)S(1)}) custom-call(s32[1,32]{1,0:T(1,128)S(1)} %constant_dynamic-slice_fusion.row, s32[1,256]{1,0:T(1,128)S(1)} %copy-done.1, ...), custom_call_target="tpu_custom_call", output_to_operand_aliasing={{0}: (8, {}), {1}: (9, {}), {2}: (10, {})} | custom-call | flops 6845104128 | bytes 1769472 | tf_op jit(solution)/shard_map/attend/pallas_call | solution.py:169
  89.7 0.1 collective-permute-start.16
  89.8 8.6 %collective-permute-done.16 = bf16[1,256,256]{2,1,0:T(8,128)(2,1)S(1)} collective-permute-done((bf16[1,256,256]{2,1,0:T(8,128)(2,1)S(1)}, bf16[1,256,256]{2,1,0:T(8,128)(2,1)S(1)}, u32[]{:S(2)}, u32[]{:S(2)}) %collective-permute-start.16) | collective-permute-done | bytes 131104 | tf_op jit(solution)/shard_map/ppermute | solution.py:240
  98.3 0.0 collective-permute-done.15
  98.3 0.9 pad_maximum_fusion.1
  (2 shorter events, 0.0 us)
Async XLA Ops:
  0.0 9.8 %copy-start = (s32[32,32]{1,0:T(8,128)S(1)}, s32[32,32]{1,0:T(8,128)}, u32[]{:S(2)}) copy-start(s32[32,32]{1,0:T(8,128)} %param.8) | copy-start | bytes 12292
  0.0 9.8 %copy-start.1 = (s32[1,256]{1,0:T(1,128)S(1)}, s32[1,256]{1,0:T(1,128)}, u32[]{:S(2)}) copy-start(s32[1,256]{1,0:T(1,128)} %ids_v.15) | copy-start | bytes 3076
  2.5 1.8 %collective-permute-start = (bf16[1,592,256]{2,1,0:T(8,128)(2,1)}, bf16[1,592,256]{2,1,0:T(8,128)(2,1)S(1)}, u32[]{:S(2)}, u32[]{:S(2)}) collective-permute-start(bf16[1,592,256]{2,1,0:T(8,128)(2,1)} %maximum_bitcast_fusion), channel_id=1, source_target_pairs={{0,8},{8,0},{16,24},{24,16},{32,40},{40,32},{48,56},{56,48},{64,72... | collective-permute-start | bytes 909320 | tf_op jit(solution)/shard_map/ppermute | solution.py:200
  5.3 11.5 %collective-permute-start.3 = (bf16[2,592,256]{2,1,0:T(8,128)(2,1)S(1)}, bf16[2,592,256]{2,1,0:T(8,128)(2,1)}, u32[]{:S(2)}, u32[]{:S(2)}) collective-permute-start(bf16[2,592,256]{2,1,0:T(8,128)(2,1)S(1)} %pad_maximum_fusion.refs_0_), channel_id=1, source_target_pairs={{0,32},{8,200},{16,48},{24,216},{32,64},{40,232},{48,80},{56,248},... | collective-permute-start | bytes 1818632 | tf_op jit(solution)/shard_map/ppermute | solution.py:204
  5.4 10.1 %collective-permute-start.1 = (bf16[1,592,256]{2,1,0:T(8,128)(2,1)}, bf16[1,592,256]{2,1,0:T(8,128)(2,1)S(1)}, u32[]{:S(2)}, u32[]{:S(2)}) collective-permute-start(bf16[1,592,256]{2,1,0:T(8,128)(2,1)} %maximum_bitcast_fusion), channel_id=1, source_target_pairs={{0,16},{8,24},{16,0},{24,8},{32,48},{40,56},{48,32},{56,40},{64,80... | collective-permute-start | bytes 909320 | tf_op jit(solution)/shard_map/ppermute | solution.py:197
  15.5 9.9 %collective-permute-start.2 = (bf16[1,592,256]{2,1,0:T(8,128)(2,1)S(1)}, bf16[1,592,256]{2,1,0:T(8,128)(2,1)S(1)}, u32[]{:S(2)}, u32[]{:S(2)}) collective-permute-start(bf16[1,592,256]{2,1,0:T(8,128)(2,1)S(1)} %collective-permute-done.1.refs_0_), channel_id=1, source_target_pairs={{0,8},{8,0},{16,24},{24,16},{32,40},{40,32},{48,56},{56,48},{64,72... | collective-permute-start | bytes 909320 | tf_op jit(solution)/shard_map/ppermute | solution.py:200
  16.9 14.2 %collective-permute-start.4 = (bf16[2,592,256]{2,1,0:T(8,128)(2,1)}, bf16[2,592,256]{2,1,0:T(8,128)(2,1)S(1)}, u32[]{:S(2)}, u32[]{:S(2)}) collective-permute-start(bf16[2,592,256]{2,1,0:T(8,128)(2,1)} %collective-permute-done.3.refs_1_), channel_id=1, source_target_pairs={{0,32},{8,232},{16,48},{24,248},{32,64},{40,8},{48,80},{56,24},{64... | collective-permute-start | bytes 1818632 | tf_op jit(solution)/shard_map/ppermute | solution.py:204
  19.2 14.0 %collective-permute-start.6 = (bf16[2,592,256]{2,1,0:T(8,128)(2,1)}, bf16[2,592,256]{2,1,0:T(8,128)(2,1)S(1)}, u32[]{:S(2)}, u32[]{:S(2)}) collective-permute-start(bf16[2,592,256]{2,1,0:T(8,128)(2,1)} %collective-permute-done.3.refs_1_), channel_id=1, source_target_pairs={{0,8},{8,0},{16,24},{24,16},{32,40},{40,32},{48,56},{56,48},{64,72... | collective-permute-start | bytes 1818632 | tf_op jit(solution)/shard_map/ppermute | solution.py:200
  22.8 16.7 %collective-permute-start.7 = (bf16[2,592,256]{2,1,0:T(8,128)(2,1)}, bf16[2,592,256]{2,1,0:T(8,128)(2,1)S(1)}, u32[]{:S(2)}, u32[]{:S(2)}) collective-permute-start(bf16[2,592,256]{2,1,0:T(8,128)(2,1)} %collective-permute-done.3.refs_1_), channel_id=1, source_target_pairs={{0,16},{8,24},{16,0},{24,8},{32,48},{40,56},{48,32},{56,40},{64,80... | collective-permute-start | bytes 1818632 | tf_op jit(solution)/shard_map/ppermute | solution.py:197
  31.1 10.3 %collective-permute-start.8 = (bf16[2,592,256]{2,1,0:T(8,128)(2,1)S(1)}, bf16[2,592,256]{2,1,0:T(8,128)(2,1)S(1)}, u32[]{:S(2)}, u32[]{:S(2)}) collective-permute-start(bf16[2,592,256]{2,1,0:T(8,128)(2,1)S(1)} %collective-permute-done.4.refs_1_), channel_id=1, source_target_pairs={{0,32},{8,232},{16,48},{24,248},{32,64},{40,8},{48,80},{56,24},{64... | collective-permute-start | bytes 1818632 | tf_op jit(solution)/shard_map/ppermute | solution.py:204
  31.3 12.4 %collective-permute-start.5 = (bf16[2,592,256]{2,1,0:T(8,128)(2,1)S(1)}, bf16[2,592,256]{2,1,0:T(8,128)(2,1)S(1)}, u32[]{:S(2)}, u32[]{:S(2)}) collective-permute-start(bf16[2,592,256]{2,1,0:T(8,128)(2,1)S(1)} %collective-permute-done.4.refs_1_), channel_id=1, source_target_pairs={{0,8},{8,0},{16,24},{24,16},{32,40},{40,32},{48,56},{56,48},{64,72... | collective-permute-start | bytes 1818632 | tf_op jit(solution)/shard_map/ppermute | solution.py:200
  41.4 17.5 %collective-permute-start.9 = (bf16[2,592,256]{2,1,0:T(8,128)(2,1)S(1)}, bf16[2,592,256]{2,1,0:T(8,128)(2,1)S(1)}, u32[]{:S(2)}, u32[]{:S(2)}) collective-permute-start(bf16[2,592,256]{2,1,0:T(8,128)(2,1)S(1)} %collective-permute-done.7.refs_1_), channel_id=1, source_target_pairs={{0,32},{8,232},{16,48},{24,248},{32,64},{40,8},{48,80},{56,24},{64... | collective-permute-start | bytes 1818632 | tf_op jit(solution)/shard_map/ppermute | solution.py:204
  42.6 16.8 %collective-permute-start.13 = (bf16[2,592,256]{2,1,0:T(8,128)(2,1)S(1)}, bf16[2,592,256]{2,1,0:T(8,128)(2,1)S(1)}, u32[]{:S(2)}, u32[]{:S(2)}) collective-permute-start(bf16[2,592,256]{2,1,0:T(8,128)(2,1)S(1)} %collective-permute-done.7.refs_1_), channel_id=1, source_target_pairs={{0,8},{8,0},{16,24},{24,16},{32,40},{40,32},{48,56},{56,48},{64,72... | collective-permute-start | bytes 1818632 | tf_op jit(solution)/shard_map/ppermute | solution.py:200
  43.2 15.6 %collective-permute-start.10 = (bf16[2,592,256]{2,1,0:T(8,128)(2,1)S(1)}, bf16[2,592,256]{2,1,0:T(8,128)(2,1)S(1)}, u32[]{:S(2)}, u32[]{:S(2)}) collective-permute-start(bf16[2,592,256]{2,1,0:T(8,128)(2,1)S(1)} %collective-permute-done.8.refs_2_), channel_id=1, source_target_pairs={{0,16},{8,24},{16,0},{24,8},{32,48},{40,56},{48,32},{56,40},{64,80... | collective-permute-start | bytes 1818632 | tf_op jit(solution)/shard_map/ppermute | solution.py:197
  43.7 15.6 %collective-permute-start.14 = (bf16[2,592,256]{2,1,0:T(8,128)(2,1)S(1)}, bf16[2,592,256]{2,1,0:T(8,128)(2,1)S(1)}, u32[]{:S(2)}, u32[]{:S(2)}) collective-permute-start(bf16[2,592,256]{2,1,0:T(8,128)(2,1)S(1)} %collective-permute-done.8.refs_2_), channel_id=1, source_target_pairs={{0,8},{8,0},{16,24},{24,16},{32,40},{40,32},{48,56},{56,48},{64,72... | collective-permute-start | bytes 1818632 | tf_op jit(solution)/shard_map/ppermute | solution.py:200
  58.8 11.6 %copy-start.2 = (bf16[1,8,512,128]{3,2,1,0:T(8,128)(2,1)S(1)}, bf16[1,8,512,128]{3,2,1,0:T(8,128)(2,1)}, u32[]{:S(2)}) copy-start(bf16[1,8,512,128]{3,2,1,0:T(8,128)(2,1)} %param.9) | copy-start | bytes 3145732
  58.8 11.5 %collective-permute-start.11 = (bf16[2,592,256]{2,1,0:T(8,128)(2,1)S(1)}, bf16[2,592,256]{2,1,0:T(8,128)(2,1)S(1)}, u32[]{:S(2)}, u32[]{:S(2)}) collective-permute-start(bf16[2,592,256]{2,1,0:T(8,128)(2,1)S(1)} %collective-permute-done.9.refs_2_), channel_id=1, source_target_pairs={{0,8},{8,0},{16,24},{24,16},{32,40},{40,32},{48,56},{56,48},{64,72... | collective-permute-start | bytes 1818632 | tf_op jit(solution)/shard_map/ppermute | solution.py:200
  58.8 11.5 %collective-permute-start.12 = (bf16[2,592,256]{2,1,0:T(8,128)(2,1)S(1)}, bf16[2,592,256]{2,1,0:T(8,128)(2,1)S(1)}, u32[]{:S(2)}, u32[]{:S(2)}) collective-permute-start(bf16[2,592,256]{2,1,0:T(8,128)(2,1)S(1)} %collective-permute-done.10.refs_1_), channel_id=1, source_target_pairs={{0,8},{8,0},{16,24},{24,16},{32,40},{40,32},{48,56},{56,48},{64,72... | collective-permute-start | bytes 1818632 | tf_op jit(solution)/shard_map/ppermute | solution.py:200
  81.7 16.7 %collective-permute-start.15 = (bf16[1,256,768]{2,1,0:T(8,128)(2,1)S(1)}, bf16[1,256,768]{2,1,0:T(8,128)(2,1)S(1)}, u32[]{:S(2)}, u32[]{:S(2)}) collective-permute-start(bf16[1,256,768]{2,1,0:T(8,128)(2,1)S(1)} %bitcast.19), channel_id=1, source_target_pairs={{0,1},{1,2},{2,3},{3,4},{4,5},{5,6},{6,7},{7,0},{8,9},{9,10},{10,1... | collective-permute-start | bytes 1179656 | tf_op jit(solution)/shard_map/ppermute | solution.py:240
  89.7 8.7 %collective-permute-start.16 = (bf16[1,256,256]{2,1,0:T(8,128)(2,1)S(1)}, bf16[1,256,256]{2,1,0:T(8,128)(2,1)S(1)}, u32[]{:S(2)}, u32[]{:S(2)}) collective-permute-start(bf16[1,256,256]{2,1,0:T(8,128)(2,1)S(1)} %bitcast.20), channel_id=1, source_target_pairs={{0,1},{1,2},{2,3},{3,4},{4,5},{5,6},{6,7},{7,0},{8,9},{9,10},{10,1... | collective-permute-start | bytes 393224 | tf_op jit(solution)/shard_map/ppermute | solution.py:240

commit v2 on v1

--- a/solution.py
+++ b/solution.py
@@ -182,6 +182,30 @@
     return list(result)
 
 
+def join(cache, ids, own, pair):
+    width = cache.shape[1]
+    rows = jnp.broadcast_to(ids[...].astype(jnp.float32), (id_rows, ids.shape[1])).astype(jnp.bfloat16)
+    for out in (own, pair):
+        out[0, 0:width, :] = cache[0]
+        out[0, width : width + id_rows, :] = rows
+
+
+def fill(other, half, pair):
+    pair[1] = other[0]
+
+
+def in_vmem(kernel, out_shape, operands, aliases):
+    vectors = pl.BlockSpec(memory_space=pltpu.VMEM)
+    return pl.pallas_call(
+        kernel,
+        out_shape=out_shape,
+        in_specs=[vectors] * len(operands),
+        out_specs=[vectors] * len(out_shape),
+        input_output_aliases=aliases,
+        compiler_params=pltpu.CompilerParams(vmem_limit_bytes=8 * 2**20),
+    )(*operands)
+
+
 def tie(*arrays):
     return list(lax.optimization_barrier(tuple(arrays)))
 
@@ -203,12 +227,22 @@
         down = 8 if step == 1 else 4
         return lax.ppermute(x, "ctx", [(i, (i + 4 if i % 2 == 0 else i - down) % devices) for i in range(devices)])
 
-    ids = jnp.broadcast_to(doc_ids.astype(jnp.bfloat16), (id_rows, tokens))
-    own = jnp.concatenate([latent_cache[0], ids], axis=0)[None]
+    rows = width + id_rows
+    own, half = in_vmem(
+        join,
+        [pltpu.VMEM((1, rows, tokens), jnp.bfloat16), pltpu.VMEM((2, rows, tokens), jnp.bfloat16)],
+        [latent_cache, doc_ids],
+        {},
+    )
     c0, x0 = core(own), across(own)
     row = lax.dynamic_slice_in_dim(block_table, me, 1, 0)
 
-    pair = jnp.concatenate([own, c0], axis=0)
+    (pair,) = in_vmem(
+        fill,
+        [pltpu.VMEM((2, rows, tokens), jnp.bfloat16)],
+        [c0, pltpu.with_memory_space_constraint(half, pltpu.VMEM)],
+        {1: 0},
+    )
     z1 = along(pair, 1)
     queries_t = pltpu.with_memory_space_constraint(queries[0].T, pltpu.VMEM)
 
@@ -228,14 +262,17 @@
     *state, x1, z3 = tie(*state, x1, z3)
     x3, xz2, cx1, cz3 = across(z3), along(x1, 2), core(x1), core(z3)
     state = run([(2, 0, 1), (1, 1, 0), (3, 0, 0)], [cz2, x1, z3], state)
-    *state, xz2, x3 = tie(*state, xz2, x3)
-    cxz2, cx3 = core(xz2), core(x3)
-    state = run([(1, 1, 1), (3, 0, 1), (2, 1, 0)], [cx1, cz3, xz2], state)
+    *state, xz2 = tie(*state, xz2)
+    cxz2 = core(xz2)
+    state = run([(1, 1, 1), (3, 0, 1)], [cx1, cz3], state)
+    *state, x3 = tie(*state, x3)
+    cx3 = core(x3)
+    state = run([(2, 1, 0), (2, 1, 1)], [xz2, cxz2], state)
     sections = lax.axis_size("section")
     handed = []
     for part in (tuple(range(heads - heads // 4)), tuple(range(heads - heads // 4, heads))):
         *state, heads_out = run(
-            [(2, 1, 1), (3, 1, 0), (3, 1, 1)], [cxz2, x3, cx3], state, w_uv[0], part
+            [(3, 1, 0), (3, 1, 1)], [x3, cx3], state, w_uv[0], part
         )
         handed.append(lax.ppermute(heads_out[None], "section", [(i, (i + 1) % sections) for i in range(sections)]))
     return jnp.concatenate(handed, axis=2)

time: 98.5 us -> 95 us (0.964)
  the two profiles are of different devices: /device:TPU:224 before, /device:TPU:193 now
where the time goes in v2:
time: 95 us; the launch traced here: 95.4 us
  Pallas kernels  54.2 us (57%)
  waiting for transfers between devices  23.3 us (25%)
  starting transfers between devices  12.4 us (13%)
  local copies, waits for them, and re-layouts  4.51 us (5%)
    pallas_call x9, Pallas kernels, stage(): pl.pallas_call(functools.partial(attend, tuple(places), first, chosen, fi...  53.4 us
    ppermute x2, waiting for transfers between devices, shards(): lax.ppermute(heads_out[None], 'section', [(i, (i + 1) % sections) for i i...  10.6 us
    ppermute x4, waiting for transfers between devices, along(): lax.ppermute(x, 'ctx', [(i, (i + 4 if i % 2 == 0 else i - down) % devices...  10.4 us
    unnamed x11, local copies, waits for them, and re-layouts  4.49 us
    ppermute x8, starting transfers between devices, core(): return lax.ppermute(x, 'ctx', [(i, i ^ 1) for i in range(devices)])  4.29 us
    ppermute x3, starting transfers between devices, across(): return lax.ppermute(x, 'ctx', [(i, i ^ 2) for i in range(devices)])  4.19 us
    ppermute x4, starting transfers between devices, along(): lax.ppermute(x, 'ctx', [(i, (i + 4 if i % 2 == 0 else i - down) % devices...  3.74 us
  transfers between devices with their start and end apart: 17, of which 6 were waited for; matrix products, arithmetic and copies ran while one was open for 3% of the time, Pallas kernels for 48%

profile of v2, /device:TPU:193, one launch (start us, length us, event | category | flops | bytes accessed | tf_op | source)
XLA Modules:
  0.0 95.4 jit_solution(1397789132916255793)
XLA Ops:
  0.0 0.0 copy-start
  0.0 0.0 copy-start.1
  0.0 1.0 %copy-done.1 = bf16[1,576,256]{2,1,0:T(8,128)(2,1)S(1)} copy-done((bf16[1,576,256]{2,1,0:T(8,128)(2,1)S(1)}, bf16[1,576,256]{2,1,0:T(8,128)(2,1)}, u32[]{:S(2)}) %copy-start.1) | copy-done | bytes 294936
  1.0 0.0 copy-start.2
  1.0 0.7 copy-done.2
  1.7 0.0 copy-start.3
  1.7 0.8 shard_map.55
  2.4 0.7 collective-permute-start
  3.1 1.4 %collective-permute-done.other = bf16[1,592,256]{2,1,0:T(8,128)(2,1)S(1)} collective-permute-done((bf16[1,592,256]{2,1,0:T(8,128)(2,1)}, bf16[1,592,256]{2,1,0:T(8,128)(2,1)S(1)}, u32[]{:S(2)}, u32[]{:S(2)}) %collective-permute-start) | collective-permute-done | bytes 303136 | tf_op jit(solution)/shard_map/ppermute | solution.py:224
  4.5 1.2 %collective-permute-start.2 = (bf16[2,592,256]{2,1,0:T(8,128)(2,1)S(1)}, bf16[2,592,256]{2,1,0:T(8,128)(2,1)}, u32[]{:S(2)}, u32[]{:S(2)}) collective-permute-start(bf16[2,592,256]{2,1,0:T(8,128)(2,1)S(1)} %shard_map.56.refs_0_), channel_id=1, source_target_pairs={{0,32},{8,200},{16,48},{24,216},{32,64},{40,232},{48,80},{56,248},... | collective-permute-start | bytes 1818632 | tf_op jit(solution)/shard_map/ppermute | solution.py:228
  5.8 1.2 %collective-permute-start.1 = (bf16[1,592,256]{2,1,0:T(8,128)(2,1)}, bf16[1,592,256]{2,1,0:T(8,128)(2,1)S(1)}, u32[]{:S(2)}, u32[]{:S(2)}) collective-permute-start(bf16[1,592,256]{2,1,0:T(8,128)(2,1)} %get-tuple-element.58), channel_id=1, source_target_pairs={{0,16},{8,24},{16,0},{24,8},{32,48},{40,56},{48,32},{56,40},{64,80... | collective-permute-start | bytes 909320 | tf_op jit(solution)/shard_map/ppermute | solution.py:221
  7.0 2.8 %copy.31 = bf16[1,256,4608]{1,2,0:T(8,128)(2,1)S(1)} copy(bf16[1,256,4608]{2,1,0:T(8,128)(2,1)} %param.5) | data formatting | bytes 4718592 | tf_op args[0]
  9.8 0.0 copy-done
  9.9 0.0 copy-done.3
  9.9 5.2 %attend.9 = (f32[8,256]{1,0:T(8,128)S(1)}, f32[8,256]{1,0:T(8,128)S(1)}, f32[8,512,256]{2,1,0:T(8,128)S(1)}) custom-call(s32[1,32]{1,0:T(1,128)S(1)} %constant_dynamic-slice_fusion.row, s32[1,256]{1,0:T(1,128)S(1)} %copy-done.3, s32[1,256]{1,0:T(1,128)S(1)} %copy-done.3, bf16[4608,256]{1,0:T(8,128)(2,1)S(1)} %bitcast.6, ...), custom_call_target="tpu_custom_call" | custom-call | flops 2281701376 | bytes 589824 | tf_op jit(solution)/shard_map/attend/pallas_call | solution.py:169
  15.1 0.0 collective-permute-done.1.refs_0_
  15.1 0.5 collective-permute-start.4
  15.6 0.7 attend.10
  16.3 3.7 %collective-permute-done.2.refs_1_ = bf16[2,592,256]{2,1,0:T(8,128)(2,1)} collective-permute-done((bf16[2,592,256]{2,1,0:T(8,128)(2,1)S(1)}, bf16[2,592,256]{2,1,0:T(8,128)(2,1)}, u32[]{:S(2)}, u32[]{:S(2)}) %collective-permute-start.2) | collective-permute-done | bytes 606240 | tf_op jit(solution)/shard_map/ppermute | solution.py:228
  20.0 1.8 %collective-permute-start.5 = (bf16[2,592,256]{2,1,0:T(8,128)(2,1)}, bf16[2,592,256]{2,1,0:T(8,128)(2,1)S(1)}, u32[]{:S(2)}, u32[]{:S(2)}) collective-permute-start(bf16[2,592,256]{2,1,0:T(8,128)(2,1)} %collective-permute-done.2.refs_1_), channel_id=1, source_target_pairs={{0,32},{8,232},{16,48},{24,248},{32,64},{40,8},{48,80},{56,24},{64... | collective-permute-start | bytes 1818632 | tf_op jit(solution)/shard_map/ppermute | solution.py:228
  21.9 0.0 collective-permute-start.3
  21.9 1.6 %collective-permute-start.6 = (bf16[2,592,256]{2,1,0:T(8,128)(2,1)}, bf16[2,592,256]{2,1,0:T(8,128)(2,1)S(1)}, u32[]{:S(2)}, u32[]{:S(2)}) collective-permute-start(bf16[2,592,256]{2,1,0:T(8,128)(2,1)} %collective-permute-done.2.refs_1_), channel_id=1, source_target_pairs={{0,16},{8,24},{16,0},{24,8},{32,48},{40,56},{48,32},{56,40},{64,80... | collective-permute-start | bytes 1818632 | tf_op jit(solution)/shard_map/ppermute | solution.py:221
  23.5 0.0 collective-permute-done.4.refs_0_
  23.5 3.7 %attend.11 = (f32[8,256]{1,0:T(8,128)S(1)}, f32[8,256]{1,0:T(8,128)S(1)}, f32[8,512,256]{2,1,0:T(8,128)S(1)}) custom-call(s32[1,32]{1,0:T(1,128)S(1)} %constant_dynamic-slice_fusion.row, s32[1,256]{1,0:T(1,128)S(1)} %copy-done.3, s32[1,256]{1,0:T(1,128)S(1)} %copy-done.3, ...), custom_call_target="tpu_custom_call", output_to_operand_aliasing={{0}: (6, {}), {1}: (7, {}), {2}: (8, {})} | custom-call | flops 3422552064 | bytes 884736 | tf_op jit(solution)/shard_map/attend/pallas_call | solution.py:169
  27.2 3.4 %collective-permute-done.5.refs_1_ = bf16[2,592,256]{2,1,0:T(8,128)(2,1)S(1)} collective-permute-done((bf16[2,592,256]{2,1,0:T(8,128)(2,1)}, bf16[2,592,256]{2,1,0:T(8,128)(2,1)S(1)}, u32[]{:S(2)}, u32[]{:S(2)}) %collective-permute-start.5) | collective-permute-done | bytes 606240 | tf_op jit(solution)/shard_map/ppermute | solution.py:228
  30.6 0.7 collective-permute-start.7
  31.3 0.0 collective-permute-start.10
  31.3 0.0 collective-permute-done.3.refs_0_
  31.3 5.1 %attend.12 = (f32[8,256]{1,0:T(8,128)S(1)}, f32[8,256]{1,0:T(8,128)S(1)}, f32[8,512,256]{2,1,0:T(8,128)S(1)}) custom-call(s32[1,32]{1,0:T(1,128)S(1)} %constant_dynamic-slice_fusion.row, s32[1,256]{1,0:T(1,128)S(1)} %copy-done.3, s32[1,256]{1,0:T(1,128)S(1)} %copy-done.3, ...), custom_call_target="tpu_custom_call", output_to_operand_aliasing={{0}: (6, {}), {1}: (7, {}), {2}: (8, {})} | custom-call | flops 4563402752 | bytes 1179648 | tf_op jit(solution)/shard_map/attend/pallas_call | solution.py:169
  36.3 0.8 collective-permute-done.6.refs_1_
  37.2 3.2 %collective-permute-done.7.refs_2_ = bf16[2,592,256]{2,1,0:T(8,128)(2,1)S(1)} collective-permute-done((bf16[2,592,256]{2,1,0:T(8,128)(2,1)S(1)}, bf16[2,592,256]{2,1,0:T(8,128)(2,1)S(1)}, u32[]{:S(2)}, u32[]{:S(2)}) %collective-permute-start.7) | collective-permute-done | bytes 606240 | tf_op jit(solution)/shard_map/ppermute | solution.py:228
  40.4 0.0 collective-permute-start.11
  40.4 0.0 collective-permute-start.8
  40.4 0.5 collective-permute-start.9
  40.9 1.4 %collective-permute-start.12 = (bf16[2,592,256]{2,1,0:T(8,128)(2,1)S(1)}, bf16[2,592,256]{2,1,0:T(8,128)(2,1)S(1)}, u32[]{:S(2)}, u32[]{:S(2)}) collective-permute-start(bf16[2,592,256]{2,1,0:T(8,128)(2,1)S(1)} %collective-permute-done.7.refs_2_), channel_id=1, source_target_pairs={{0,16},{8,24},{16,0},{24,8},{32,48},{40,56},{48,32},{56,40},{64,80... | collective-permute-start | bytes 1818632 | tf_op jit(solution)/shard_map/ppermute | solution.py:221
  42.3 0.0 collective-permute-done.10.refs_0_
  42.3 12.7 %attend.13 = (f32[8,256]{1,0:T(8,128)S(1)}, f32[8,256]{1,0:T(8,128)S(1)}, f32[8,512,256]{2,1,0:T(8,128)S(1)}) custom-call(s32[1,32]{1,0:T(1,128)S(1)} %constant_dynamic-slice_fusion.row, s32[1,256]{1,0:T(1,128)S(1)} %copy-done.3, s32[1,256]{1,0:T(1,128)S(1)} %copy-done.3, ...), custom_call_target="tpu_custom_call", output_to_operand_aliasing={{0}: (7, {}), {1}: (8, {}), {2}: (9, {})} | custom-call | flops 6845104128 | bytes 1769472 | tf_op jit(solution)/shard_map/attend/pallas_call | solution.py:169
  55.0 0.0 collective-permute-done.11.refs_0_
  55.0 0.1 collective-permute-start.14
  55.1 0.0 collective-permute-done.8.refs_0_
  55.1 0.0 collective-permute-done.9.refs_1_
  55.2 5.1 %attend.14 = (f32[8,256]{1,0:T(8,128)S(1)}, f32[8,256]{1,0:T(8,128)S(1)}, f32[8,512,256]{2,1,0:T(8,128)S(1)}) custom-call(s32[1,32]{1,0:T(1,128)S(1)} %constant_dynamic-slice_fusion.row, s32[1,256]{1,0:T(1,128)S(1)} %copy-done.3, s32[1,256]{1,0:T(1,128)S(1)} %copy-done.3, ...), custom_call_target="tpu_custom_call", output_to_operand_aliasing={{0}: (6, {}), {1}: (7, {}), {2}: (8, {})} | custom-call | flops 4563402752 | bytes 1179648 | tf_op jit(solution)/shard_map/attend/pallas_call | solution.py:169
  60.2 0.0 collective-permute-done.12.refs_0_
  60.2 0.0 copy-start.4
  60.2 2.5 %collective-permute-start.13 = (bf16[2,592,256]{2,1,0:T(8,128)(2,1)S(1)}, bf16[2,592,256]{2,1,0:T(8,128)(2,1)S(1)}, u32[]{:S(2)}, u32[]{:S(2)}) collective-permute-start(bf16[2,592,256]{2,1,0:T(8,128)(2,1)S(1)} %collective-permute-done.12.refs_0_), channel_id=1, source_target_pairs={{0,8},{8,0},{16,24},{24,16},{32,40},{40,32},{48,56},{56,48},{64,72... | collective-permute-start | bytes 1818632 | tf_op jit(solution)/shard_map/ppermute | solution.py:224
  62.7 0.0 collective-permute-done.14.refs_1_
  62.7 9.1 %attend.15 = (f32[8,256]{1,0:T(8,128)S(1)}, f32[8,256]{1,0:T(8,128)S(1)}, f32[8,512,256]{2,1,0:T(8,128)S(1)}) custom-call(s32[1,32]{1,0:T(1,128)S(1)} %constant_dynamic-slice_fusion.row, s32[1,256]{1,0:T(1,128)S(1)} %copy-done.3, s32[1,256]{1,0:T(1,128)S(1)} %copy-done.3, ...), custom_call_target="tpu_custom_call", output_to_operand_aliasing={{0}: (6, {}), {1}: (7, {}), {2}: (8, {})} | custom-call | flops 4563402752 | bytes 1179648 | tf_op jit(solution)/shard_map/attend/pallas_call | solution.py:169
  71.8 0.0 collective-permute-done.13.refs_1_
  71.8 0.0 copy-done.4
  71.8 7.8 %attend.16 = (f32[8,256]{1,0:T(8,128)S(1)}, f32[8,256]{1,0:T(8,128)S(1)}, f32[8,512,256]{2,1,0:T(8,128)S(1)}, bf16[256,768]{1,0:T(8,128)(2,1)S(1)}) custom-call(s32[1,32]{1,0:T(1,128)S(1)} %constant_dynamic-slice_fusion.row, s32[1,256]{1,0:T(1,128)S(1)} %copy-done.3, ...), custom_call_target="tpu_custom_call", output_to_operand_aliasing={{0}: (7, {}), {1}: (8, {}), {2}: (9, {})} | custom-call | flops 4563402752 | bytes 1179648 | tf_op jit(solution)/shard_map/attend/pallas_call | solution.py:169
  79.7 0.1 collective-permute-start.15
  79.8 4.0 %attend.17 = (f32[8,256]{1,0:T(8,128)S(1)}, f32[8,256]{1,0:T(8,128)S(1)}, f32[8,512,256]{2,1,0:T(8,128)S(1)}, bf16[256,256]{1,0:T(8,128)(2,1)S(1)}) custom-call(s32[1,32]{1,0:T(1,128)S(1)} %constant_dynamic-slice_fusion.row, s32[1,256]{1,0:T(1,128)S(1)} %copy-done.3, ...), custom_call_target="tpu_custom_call", output_to_operand_aliasing={{0}: (7, {}), {1}: (8, {}), {2}: (9, {})} | custom-call | flops 4563402752 | bytes 1179648 | tf_op jit(solution)/shard_map/attend/pallas_call | solution.py:169
  83.8 0.1 collective-permute-start.16
  83.9 10.6 %collective-permute-done.16 = bf16[1,256,256]{2,1,0:T(8,128)(2,1)S(1)} collective-permute-done((bf16[1,256,256]{2,1,0:T(8,128)(2,1)S(1)}, bf16[1,256,256]{2,1,0:T(8,128)(2,1)S(1)}, u32[]{:S(2)}, u32[]{:S(2)}) %collective-permute-start.16) | collective-permute-done | bytes 131104 | tf_op jit(solution)/shard_map/ppermute | solution.py:277
  94.5 0.0 collective-permute-done.15
  94.5 0.9 pad_maximum_fusion
  (2 shorter events, 0.0 us)
Async XLA Ops:
  0.0 9.8 %copy-start = (s32[32,32]{1,0:T(8,128)S(1)}, s32[32,32]{1,0:T(8,128)}, u32[]{:S(2)}) copy-start(s32[32,32]{1,0:T(8,128)} %param.8) | copy-start | bytes 12292
  0.0 1.0 %copy-start.1 = (bf16[1,576,256]{2,1,0:T(8,128)(2,1)S(1)}, bf16[1,576,256]{2,1,0:T(8,128)(2,1)}, u32[]{:S(2)}) copy-start(bf16[1,576,256]{2,1,0:T(8,128)(2,1)} %cache.1) | copy-start | bytes 884740
  1.0 0.7 copy-start.2
  1.7 8.2 %copy-start.3 = (s32[1,256]{1,0:T(1,128)S(1)}, s32[1,256]{1,0:T(1,128)}, u32[]{:S(2)}) copy-start(s32[1,256]{1,0:T(1,128)} %ids_v.17) | copy-start | bytes 3076
  2.4 2.1 %collective-permute-start = (bf16[1,592,256]{2,1,0:T(8,128)(2,1)}, bf16[1,592,256]{2,1,0:T(8,128)(2,1)S(1)}, u32[]{:S(2)}, u32[]{:S(2)}) collective-permute-start(bf16[1,592,256]{2,1,0:T(8,128)(2,1)} %get-tuple-element.58), channel_id=1, source_target_pairs={{0,8},{8,0},{16,24},{24,16},{32,40},{40,32},{48,56},{56,48},{64,72... | collective-permute-start | bytes 909320 | tf_op jit(solution)/shard_map/ppermute | solution.py:224
  4.5 15.5 %collective-permute-start.2 = (bf16[2,592,256]{2,1,0:T(8,128)(2,1)S(1)}, bf16[2,592,256]{2,1,0:T(8,128)(2,1)}, u32[]{:S(2)}, u32[]{:S(2)}) collective-permute-start(bf16[2,592,256]{2,1,0:T(8,128)(2,1)S(1)} %shard_map.56.refs_0_), channel_id=1, source_target_pairs={{0,32},{8,200},{16,48},{24,216},{32,64},{40,232},{48,80},{56,248},... | collective-permute-start | bytes 1818632 | tf_op jit(solution)/shard_map/ppermute | solution.py:228
  5.8 9.3 %collective-permute-start.1 = (bf16[1,592,256]{2,1,0:T(8,128)(2,1)}, bf16[1,592,256]{2,1,0:T(8,128)(2,1)S(1)}, u32[]{:S(2)}, u32[]{:S(2)}) collective-permute-start(bf16[1,592,256]{2,1,0:T(8,128)(2,1)} %get-tuple-element.58), channel_id=1, source_target_pairs={{0,16},{8,24},{16,0},{24,8},{32,48},{40,56},{48,32},{56,40},{64,80... | collective-permute-start | bytes 909320 | tf_op jit(solution)/shard_map/ppermute | solution.py:221
  15.1 8.4 %collective-permute-start.4 = (bf16[1,592,256]{2,1,0:T(8,128)(2,1)S(1)}, bf16[1,592,256]{2,1,0:T(8,128)(2,1)S(1)}, u32[]{:S(2)}, u32[]{:S(2)}) collective-permute-start(bf16[1,592,256]{2,1,0:T(8,128)(2,1)S(1)} %collective-permute-done.1.refs_0_), channel_id=1, source_target_pairs={{0,8},{8,0},{16,24},{24,16},{32,40},{40,32},{48,56},{56,48},{64,72... | collective-permute-start | bytes 909320 | tf_op jit(solution)/shard_map/ppermute | solution.py:224
  20.0 10.5 %collective-permute-start.5 = (bf16[2,592,256]{2,1,0:T(8,128)(2,1)}, bf16[2,592,256]{2,1,0:T(8,128)(2,1)S(1)}, u32[]{:S(2)}, u32[]{:S(2)}) collective-permute-start(bf16[2,592,256]{2,1,0:T(8,128)(2,1)} %collective-permute-done.2.refs_1_), channel_id=1, source_target_pairs={{0,32},{8,232},{16,48},{24,248},{32,64},{40,8},{48,80},{56,24},{64... | collective-permute-start | bytes 1818632 | tf_op jit(solution)/shard_map/ppermute | solution.py:228
  21.9 9.4 %collective-permute-start.3 = (bf16[2,592,256]{2,1,0:T(8,128)(2,1)}, bf16[2,592,256]{2,1,0:T(8,128)(2,1)S(1)}, u32[]{:S(2)}, u32[]{:S(2)}) collective-permute-start(bf16[2,592,256]{2,1,0:T(8,128)(2,1)} %collective-permute-done.2.refs_1_), channel_id=1, source_target_pairs={{0,8},{8,0},{16,24},{24,16},{32,40},{40,32},{48,56},{56,48},{64,72... | collective-permute-start | bytes 1818632 | tf_op jit(solution)/shard_map/ppermute | solution.py:224
  21.9 15.3 %collective-permute-start.6 = (bf16[2,592,256]{2,1,0:T(8,128)(2,1)}, bf16[2,592,256]{2,1,0:T(8,128)(2,1)S(1)}, u32[]{:S(2)}, u32[]{:S(2)}) collective-permute-start(bf16[2,592,256]{2,1,0:T(8,128)(2,1)} %collective-permute-done.2.refs_1_), channel_id=1, source_target_pairs={{0,16},{8,24},{16,0},{24,8},{32,48},{40,56},{48,32},{56,40},{64,80... | collective-permute-start | bytes 1818632 | tf_op jit(solution)/shard_map/ppermute | solution.py:221
  30.6 9.8 %collective-permute-start.7 = (bf16[2,592,256]{2,1,0:T(8,128)(2,1)S(1)}, bf16[2,592,256]{2,1,0:T(8,128)(2,1)S(1)}, u32[]{:S(2)}, u32[]{:S(2)}) collective-permute-start(bf16[2,592,256]{2,1,0:T(8,128)(2,1)S(1)} %collective-permute-done.5.refs_1_), channel_id=1, source_target_pairs={{0,32},{8,232},{16,48},{24,248},{32,64},{40,8},{48,80},{56,24},{64... | collective-permute-start | bytes 1818632 | tf_op jit(solution)/shard_map/ppermute | solution.py:228
  31.3 11.0 %collective-permute-start.10 = (bf16[2,592,256]{2,1,0:T(8,128)(2,1)S(1)}, bf16[2,592,256]{2,1,0:T(8,128)(2,1)S(1)}, u32[]{:S(2)}, u32[]{:S(2)}) collective-permute-start(bf16[2,592,256]{2,1,0:T(8,128)(2,1)S(1)} %collective-permute-done.5.refs_1_), channel_id=1, source_target_pairs={{0,8},{8,0},{16,24},{24,16},{32,40},{40,32},{48,56},{56,48},{64,72... | collective-permute-start | bytes 1818632 | tf_op jit(solution)/shard_map/ppermute | solution.py:224
  40.4 14.6 %collective-permute-start.11 = (bf16[2,592,256]{2,1,0:T(8,128)(2,1)S(1)}, bf16[2,592,256]{2,1,0:T(8,128)(2,1)S(1)}, u32[]{:S(2)}, u32[]{:S(2)}) collective-permute-start(bf16[2,592,256]{2,1,0:T(8,128)(2,1)S(1)} %collective-permute-done.6.refs_1_), channel_id=1, source_target_pairs={{0,32},{8,232},{16,48},{24,248},{32,64},{40,8},{48,80},{56,24},{64... | collective-permute-start | bytes 1818632 | tf_op jit(solution)/shard_map/ppermute | solution.py:228
  40.4 14.7 %collective-permute-start.8 = (bf16[2,592,256]{2,1,0:T(8,128)(2,1)S(1)}, bf16[2,592,256]{2,1,0:T(8,128)(2,1)S(1)}, u32[]{:S(2)}, u32[]{:S(2)}) collective-permute-start(bf16[2,592,256]{2,1,0:T(8,128)(2,1)S(1)} %collective-permute-done.6.refs_1_), channel_id=1, source_target_pairs={{0,8},{8,0},{16,24},{24,16},{32,40},{40,32},{48,56},{56,48},{64,72... | collective-permute-start | bytes 1818632 | tf_op jit(solution)/shard_map/ppermute | solution.py:224
  40.4 14.7 %collective-permute-start.9 = (bf16[2,592,256]{2,1,0:T(8,128)(2,1)S(1)}, bf16[2,592,256]{2,1,0:T(8,128)(2,1)S(1)}, u32[]{:S(2)}, u32[]{:S(2)}) collective-permute-start(bf16[2,592,256]{2,1,0:T(8,128)(2,1)S(1)} %collective-permute-done.7.refs_2_), channel_id=1, source_target_pairs={{0,8},{8,0},{16,24},{24,16},{32,40},{40,32},{48,56},{56,48},{64,72... | collective-permute-start | bytes 1818632 | tf_op jit(solution)/shard_map/ppermute | solution.py:224
  40.9 19.3 %collective-permute-start.12 = (bf16[2,592,256]{2,1,0:T(8,128)(2,1)S(1)}, bf16[2,592,256]{2,1,0:T(8,128)(2,1)S(1)}, u32[]{:S(2)}, u32[]{:S(2)}) collective-permute-start(bf16[2,592,256]{2,1,0:T(8,128)(2,1)S(1)} %collective-permute-done.7.refs_2_), channel_id=1, source_target_pairs={{0,16},{8,24},{16,0},{24,8},{32,48},{40,56},{48,32},{56,40},{64,80... | collective-permute-start | bytes 1818632 | tf_op jit(solution)/shard_map/ppermute | solution.py:221
  55.0 7.7 %collective-permute-start.14 = (bf16[2,592,256]{2,1,0:T(8,128)(2,1)S(1)}, bf16[2,592,256]{2,1,0:T(8,128)(2,1)S(1)}, u32[]{:S(2)}, u32[]{:S(2)}) collective-permute-start(bf16[2,592,256]{2,1,0:T(8,128)(2,1)S(1)} %collective-permute-done.11.refs_0_), channel_id=1, source_target_pairs={{0,8},{8,0},{16,24},{24,16},{32,40},{40,32},{48,56},{56,48},{64,72... | collective-permute-start | bytes 1818632 | tf_op jit(solution)/shard_map/ppermute | solution.py:224
  60.2 11.6 %copy-start.4 = (bf16[1,8,512,128]{3,2,1,0:T(8,128)(2,1)S(1)}, bf16[1,8,512,128]{3,2,1,0:T(8,128)(2,1)}, u32[]{:S(2)}) copy-start(bf16[1,8,512,128]{3,2,1,0:T(8,128)(2,1)} %param.9) | copy-start | bytes 3145732
  60.2 11.6 %collective-permute-start.13 = (bf16[2,592,256]{2,1,0:T(8,128)(2,1)S(1)}, bf16[2,592,256]{2,1,0:T(8,128)(2,1)S(1)}, u32[]{:S(2)}, u32[]{:S(2)}) collective-permute-start(bf16[2,592,256]{2,1,0:T(8,128)(2,1)S(1)} %collective-permute-done.12.refs_0_), channel_id=1, source_target_pairs={{0,8},{8,0},{16,24},{24,16},{32,40},{40,32},{48,56},{56,48},{64,72... | collective-permute-start | bytes 1818632 | tf_op jit(solution)/shard_map/ppermute | solution.py:224
  79.7 14.8 %collective-permute-start.15 = (bf16[1,256,768]{2,1,0:T(8,128)(2,1)S(1)}, bf16[1,256,768]{2,1,0:T(8,128)(2,1)S(1)}, u32[]{:S(2)}, u32[]{:S(2)}) collective-permute-start(bf16[1,256,768]{2,1,0:T(8,128)(2,1)S(1)} %bitcast.17), channel_id=1, source_target_pairs={{0,1},{1,2},{2,3},{3,4},{4,5},{5,6},{6,7},{7,0},{8,9},{9,10},{10,1... | collective-permute-start | bytes 1179656 | tf_op jit(solution)/shard_map/ppermute | solution.py:277
  83.8 10.7 %collective-permute-start.16 = (bf16[1,256,256]{2,1,0:T(8,128)(2,1)S(1)}, bf16[1,256,256]{2,1,0:T(8,128)(2,1)S(1)}, u32[]{:S(2)}, u32[]{:S(2)}) collective-permute-start(bf16[1,256,256]{2,1,0:T(8,128)(2,1)S(1)} %bitcast.18), channel_id=1, source_target_pairs={{0,1},{1,2},{2,3},{3,4},{4,5},{5,6},{6,7},{7,0},{8,9},{9,10},{10,1... | collective-permute-start | bytes 393224 | tf_op jit(solution)/shard_map/ppermute | solution.py:277
